TPU v7x, 32 devices: a whole 2x2x4 slice. The times are simulated.
32 devices in a mesh: dp: 8 (over z, y), mp: 4 (over x, core).
Axes of the slice: x: 2, y: 2, z: 4, core: 2. Of those that a mesh axis runs over, the one named last changes fastest.
Arguments:
- byte_embeds: bfloat16 [4, 4096, 1024], P('mp', 'dp'), may hold values from -6 to 6
- lengths: int32 [4], replicated, may hold values from 3585 to 4096, as said below
- patch_in: bfloat16 [8388608], P(('dp', 'mp')), may hold values from -0.0625 to 0.0625
- mixer_in: bfloat16 [4489216], P(('dp', 'mp')), may hold values from -0.1875 to 0.1875
- mixer_out: bfloat16 [2097152], P(('dp', 'mp')), may hold values from -0.125 to 0.125
- patch_out: bfloat16 [8388608], P(('dp', 'mp')), may hold values from -0.1875 to 0.1875
- attend_in: bfloat16 [3145728], P(('dp', 'mp')), may hold values from -0.1875 to 0.1875
- attend_out: bfloat16 [1048576], P(('dp', 'mp')), may hold values from -0.375 to 0.375
- gate_weight: bfloat16 [1024, 4096], P('dp', 'mp'), may hold values from -0.1875 to 0.1875
- up_weight: bfloat16 [1024, 4096], P('dp', 'mp'), may hold values from -0.1875 to 0.1875
- down_weight: bfloat16 [4096, 1024], P('mp', 'dp'), may hold values from -0.09375 to 0.09375
- norm_global: float32 [1024], replicated, may hold values from 0.25 to 1.75
- conv_weight: float32 [4, 2304], replicated, may hold values from -3 to 3
- conv_bias: float32 [2304], replicated, may hold values from -3 to 3
- step_bias: float32 [32], replicated, may hold values from -1 to 1
- decay_rate: float32 [32], replicated, may hold values from -8 to -1
- skip_gain: float32 [32], replicated, may hold values from 0.5 to 1.5
- norm_gated: float32 [2048], replicated, may hold values from 0.25 to 1.75
- norm_attend: float32 [1024], replicated, may hold values from 0.25 to 1.75
- norm_feed: float32 [1024], replicated, may hold values from 0.25 to 1.75
- cotangent: bfloat16 [4, 4096, 1024], P('mp', 'dp'), may hold values from -6 to 6
Outputs:
- out_bytes: bfloat16 [4, 4096, 1024], P('mp', 'dp')
- grad_bytes: bfloat16 [4, 4096, 1024], P('mp', 'dp')
- grad_patch_in: float32 [8388608], P(('dp', 'mp'))
- grad_mixer_in: float32 [4489216], P(('dp', 'mp'))
- grad_mixer_out: float32 [2097152], P(('dp', 'mp'))
- grad_patch_out: float32 [8388608], P(('dp', 'mp'))
- grad_attend_in: float32 [3145728], P(('dp', 'mp'))
- grad_attend_out: float32 [1048576], P(('dp', 'mp'))
- grad_gate: float32 [1024, 4096], P('dp', 'mp')
- grad_up: float32 [1024, 4096], P('dp', 'mp')
- grad_down: float32 [4096, 1024], P('mp', 'dp')
- grad_norm_global: float32 [1024], replicated
- grad_conv_weight: float32 [4, 2304], replicated
- grad_conv_bias: float32 [2304], replicated
- grad_step_bias: float32 [32], replicated
- grad_decay_rate: float32 [32], replicated
- grad_skip_gain: float32 [32], replicated
- grad_norm_gated: float32 [2048], replicated
- grad_norm_attend: float32 [1024], replicated
- grad_norm_feed: float32 [1024], replicated
Inputs may be any that keep to these rules, and one draw needn't show every extreme that they name: `lengths`: every sequence uses more than its first (7) * 512 bytes; one sequence uses all 4096.
All inputs are finite; a program needn't handle non-finite values.
Results may differ from a plain program's by a relative error of at most 0.024.
Values may be sent and summed in bfloat16 or wider, within the bound.
A program may use at most 448 MiB of HBM per device.

v0:
```python
import jax
import jax.numpy as jnp
from jax import lax
from jax.sharding import PartitionSpec as P

D = 1024
PATCH = 8
INNER = 2048
HEADS_M = 32
STATE = 128
CONV = 4
HEADS_A = 16
HEAD_M = 64
HEAD_A = 64
PROJ = 4384


HIGH = lax.Precision.HIGHEST
EPSILON = 1e-05


def passed_along(value, axis, steps):
    count = lax.axis_size(axis)
    first, last = (max(0, -steps), min(count, count - steps))
    return lax.ppermute(value, axis, [(source, source + steps) for source in range(first, last)])


def entering(x, axis, join, neutral):
    place = lax.axis_index(axis)
    gathered = jax.tree.map(
        lambda a, kind: lax.all_gather(a.astype(kind), axis), x, (jnp.bfloat16, jnp.bfloat16)
    )
    state = jax.tree.map(lambda a, e: jnp.zeros_like(a) + jnp.asarray(e, a.dtype), x, neutral)

    def one(hop, state):
        return join(
            state,
            jax.tree.map(
                lambda a, own: lax.dynamic_index_in_dim(a, hop, 0, False).astype(own.dtype),
                gathered,
                x,
            ),
        )

    return lax.fori_loop(0, place, one, state)


def prefix(x, axis, combine, identity):
    devices, position = (lax.axis_size(axis), lax.axis_index(axis))
    everything = jax.tree.map(
        lambda part, kind: lax.all_gather(part.astype(kind), axis),
        x,
        jax.tree.map(lambda a: jnp.bfloat16 if a.dtype == jnp.float32 else a.dtype, x),
    )
    start = jax.tree.map(
        lambda part, zero: jnp.broadcast_to(jnp.asarray(zero, part.dtype), part.shape), x, identity
    )

    def hop(k, before):
        at = devices - 1 - k
        reached = at > position
        new = combine(
            before, jax.tree.map(lambda part, own: part[at].astype(own.dtype), everything, x)
        )
        return jax.tree.map(lambda a, b: jnp.where(reached, a, b), new, before)

    return lax.fori_loop(0, devices, hop, start)


def product(left, right):
    return jnp.dot(left, right, preferred_element_type=jnp.float32)


def left_product(left, right):
    return lax.dot_general(
        left, right, (((0,), (0,)), ((), ())), preferred_element_type=jnp.float32
    )


def right_product(left, right):
    return lax.dot_general(
        left, right, (((1,), (1,)), ((), ())), preferred_element_type=jnp.float32
    )


def root_norm(values, gain):
    return values * lax.rsqrt(jnp.mean(values * values, axis=-1, keepdims=True) + EPSILON) * gain


def convolve(extended, conv_weight, conv_bias):
    count = extended.shape[0] - (CONV - 1)
    total = conv_bias + conv_weight[0] * extended[0:count]
    for shift in range(1, CONV):
        total = total + conv_weight[shift] * extended[shift : shift + count]
    return jax.nn.silu(total)


def mixer_inputs(extended, step_raw, conv_weight, conv_bias, step_bias, decay_rate):
    activated = convolve(extended, conv_weight, conv_bias)
    count = activated.shape[0]
    heads_x = activated[:, :INNER].reshape(count, HEADS_M, HEAD_M)
    input_map = activated[:, INNER : INNER + STATE]
    output_map = activated[:, INNER + STATE :]
    step_size = jax.nn.softplus(step_raw + step_bias)
    log_decay = jnp.cumsum(step_size * -jnp.exp(decay_rate), axis=0)
    return (heads_x, input_map, output_map, step_size, log_decay)


def block_output(heads_x, input_map, output_map, step_size, log_decay, carried):
    count = log_decay.shape[0]
    decay_t = log_decay.T
    spread = decay_t[:, :, None] - decay_t[:, None, :]
    causal = jnp.arange(count)[:, None] >= jnp.arange(count)[None, :]
    factor = jnp.exp(jnp.where(causal[None], spread, -jnp.inf))
    scores = jnp.dot(output_map, input_map.T, precision=HIGH)
    weights = factor * scores[None] * step_size.T[:, None, :]
    inner = jnp.einsum("hts,shp->thp", weights, heads_x, precision=HIGH)
    outer = (
        jnp.einsum("tn,hpn->thp", output_map, carried, precision=HIGH)
        * jnp.exp(log_decay)[:, :, None]
    )
    return inner + outer


def block_state(heads_x, input_map, step_size, log_decay):
    last = log_decay[-1]
    weight = jnp.exp(last[None, :] - log_decay) * step_size
    own = jnp.einsum("sh,shp,sn->hpn", weight, heads_x, input_map, precision=HIGH)
    return (jnp.exp(last), own)


def mixer_output(
    heads_x, input_map, output_map, step_size, log_decay, carried, gate_part, skip_gain, norm_gated
):
    count = heads_x.shape[0]
    values = block_output(heads_x, input_map, output_map, step_size, log_decay, carried)
    values = values + skip_gain[None, :, None] * heads_x
    gated = values.reshape(count, INNER) * jax.nn.silu(gate_part)
    return root_norm(gated, norm_gated)


def combine_carry(earlier, later):
    return (earlier[0] * later[0], later[0][:, None, None] * earlier[1] + later[1])


def patch_attention(attend_proj):
    count = attend_proj.shape[0]
    patches = count // PATCH
    query = attend_proj[:, :D].reshape(patches, PATCH, HEADS_A, HEAD_A)
    keyed = attend_proj[:, D : 2 * D].reshape(patches, PATCH, HEADS_A, HEAD_A)
    valued = attend_proj[:, 2 * D :].reshape(patches, PATCH, HEADS_A, HEAD_A)
    scores = jnp.einsum("pihd,pjhd->phij", query, keyed, precision=HIGH) * HEAD_A ** (-0.5)
    causal = jnp.arange(PATCH)[:, None] >= jnp.arange(PATCH)[None, :]
    scores = jnp.where(causal, scores, -jnp.inf)
    top = jnp.max(scores, axis=-1, keepdims=True)
    expo = jnp.exp(scores - top)
    probs = expo / jnp.sum(expo, axis=-1, keepdims=True)
    result = jnp.einsum("phij,pjhd->pihd", probs, valued, precision=HIGH)
    return result.reshape(count, D)


def fetch_weights(patch_in, mixer_in, mixer_out, patch_out, attend_in, attend_out):
    gathered = (
        lax.all_gather(patch_in, ("dp", "mp"), axis=0, tiled=True),
        lax.all_gather(mixer_in, ("dp", "mp"), axis=0, tiled=True),
        lax.all_gather(mixer_out, ("dp", "mp"), axis=0, tiled=True),
        lax.all_gather(patch_out, ("dp", "mp"), axis=0, tiled=True),
        lax.all_gather(attend_in, ("dp", "mp"), axis=0, tiled=True),
        lax.all_gather(attend_out, ("dp", "mp"), axis=0, tiled=True),
    )
    return (
        gathered[0].reshape(PATCH * D, D),
        gathered[1].reshape(D, PROJ),
        gathered[2].reshape(INNER, D),
        gathered[3].reshape(D, PATCH * D),
        gathered[4].reshape(D, 3 * D),
        gathered[5].reshape(D, D),
    )


def body(
    byte_embeds,
    lengths,
    patch_in,
    mixer_in,
    mixer_out,
    patch_out,
    attend_in,
    attend_out,
    gate_weight,
    up_weight,
    down_weight,
    norm_global,
    conv_weight,
    conv_bias,
    step_bias,
    decay_rate,
    skip_gain,
    norm_gated,
    norm_attend,
    norm_feed,
    cotangent,
):
    rows = byte_embeds.shape[1]
    patches = rows // PATCH
    group = lax.axis_index("mp")
    place = lax.axis_index("dp")
    length = jnp.sum(jnp.where(jnp.arange(lengths.shape[0], dtype=jnp.int32) == group, lengths, 0))
    position = place * rows + jnp.arange(rows, dtype=jnp.int32)
    keep = (position < length).astype(jnp.float32)[:, None]
    inputs = byte_embeds[0].astype(jnp.float32) * keep
    patch_rows = inputs.astype(jnp.bfloat16).reshape(patches, PATCH * D)
    w_patch_in, w_mixer_in, w_mixer_out, w_patch_out, w_attend, w_attend_out = fetch_weights(
        patch_in, mixer_in, mixer_out, patch_out, attend_in, attend_out
    )
    w_gate, w_up, w_down = (
        lax.all_gather(gate_weight, "dp", axis=0, tiled=True),
        lax.all_gather(up_weight, "dp", axis=0, tiled=True),
        lax.all_gather(down_weight, "dp", axis=1, tiled=True),
    )
    global_in = product(patch_rows, w_patch_in)
    normed_low = root_norm(global_in, norm_global).astype(jnp.bfloat16)
    projected = product(normed_low, w_mixer_in)
    gate_part = projected[:, :INNER]
    conv_input = projected[:, INNER : 2 * INNER + 2 * STATE]
    step_raw = projected[:, 2 * INNER + 2 * STATE :]
    rim = passed_along(conv_input[patches - (CONV - 1) :], "dp", 1)
    extended = jnp.concatenate([rim, conv_input], axis=0)
    heads_x, input_map, output_map, step_size, log_decay = mixer_inputs(
        extended, step_raw, conv_weight, conv_bias, step_bias, decay_rate
    )
    decay_all, own_state = block_state(heads_x, input_map, step_size, log_decay)
    identity = (jnp.ones_like(decay_all), jnp.zeros_like(own_state))
    _, carried = entering((decay_all, own_state), "dp", combine_carry, identity)
    mixed = mixer_output(
        heads_x,
        input_map,
        output_map,
        step_size,
        log_decay,
        carried,
        gate_part,
        skip_gain,
        norm_gated,
    )
    mixed_low = mixed.astype(jnp.bfloat16)
    global_out = global_in + product(mixed_low, w_mixer_out)
    global_low = global_out.astype(jnp.bfloat16)
    local_in = inputs + product(global_low, w_patch_out).reshape(rows, D)
    attend_low = root_norm(local_in, norm_attend).astype(jnp.bfloat16)
    attend_proj = product(attend_low, w_attend)
    attended_low = patch_attention(attend_proj).astype(jnp.bfloat16)
    after_attend = local_in + product(attended_low, w_attend_out)
    feed_low = root_norm(after_attend, norm_feed).astype(jnp.bfloat16)
    feed_rows = lax.all_gather(feed_low, "mp", axis=0, tiled=True)
    gate_value = product(feed_rows, w_gate)
    up_value = product(feed_rows, w_up)
    sigmoid_gate = jax.nn.sigmoid(gate_value)
    silu_gate = gate_value * sigmoid_gate
    hidden_low = (silu_gate * up_value).astype(jnp.bfloat16)
    feed_out = lax.psum_scatter(
        product(hidden_low, w_down).astype(jnp.bfloat16), "mp", scatter_dimension=0, tiled=True
    ).astype(jnp.float32)
    final = after_attend + feed_out
    out_bytes = (final * keep).astype(jnp.bfloat16)[None]
    w_patch_in, w_mixer_in, w_mixer_out, w_patch_out, w_attend, w_attend_out = fetch_weights(
        patch_in, mixer_in, mixer_out, patch_out, attend_in, attend_out
    )
    grad_final = cotangent[0].astype(jnp.float32) * keep
    grad_feed_low = grad_final.astype(jnp.bfloat16)
    grad_feed_rows = lax.all_gather(grad_feed_low, "mp", axis=0, tiled=True)
    grad_hidden = right_product(grad_feed_rows, w_down)
    grad_down = left_product(hidden_low, grad_feed_rows)
    grad_gate_low = (
        grad_hidden * up_value * sigmoid_gate * (1.0 + gate_value * (1.0 - sigmoid_gate))
    ).astype(jnp.bfloat16)
    grad_up_low = (grad_hidden * silu_gate).astype(jnp.bfloat16)
    grad_gate = left_product(feed_rows, grad_gate_low)
    grad_up = left_product(feed_rows, grad_up_low)
    grad_feed_normed = lax.psum_scatter(
        (right_product(grad_gate_low, w_gate) + right_product(grad_up_low, w_up)).astype(
            jnp.bfloat16
        ),
        "mp",
        scatter_dimension=0,
        tiled=True,
    ).astype(jnp.float32)
    grad_gate, grad_up, grad_down = (
        lax.psum_scatter(
            grad_gate.astype(jnp.bfloat16), "dp", scatter_dimension=0, tiled=True
        ).astype(jnp.float32),
        lax.psum_scatter(
            grad_up.astype(jnp.bfloat16), "dp", scatter_dimension=0, tiled=True
        ).astype(jnp.float32),
        lax.psum_scatter(
            grad_down.astype(jnp.bfloat16), "dp", scatter_dimension=1, tiled=True
        ).astype(jnp.float32),
    )
    _, pull_feed = jax.vjp(root_norm, after_attend, norm_feed)
    grad_after_norm, grad_norm_feed = pull_feed(grad_feed_normed)
    grad_after = grad_final + grad_after_norm
    grad_attend_low = grad_after.astype(jnp.bfloat16)
    grad_attend_out = left_product(attended_low, grad_attend_low)
    grad_attended = right_product(grad_attend_low, w_attend_out)
    _, pull_attend = jax.vjp(patch_attention, attend_proj)
    (grad_proj,) = pull_attend(grad_attended)
    grad_proj_low = grad_proj.astype(jnp.bfloat16)
    grad_attend_in = left_product(attend_low, grad_proj_low)
    grad_attend_normed = right_product(grad_proj_low, w_attend)
    _, pull_local = jax.vjp(root_norm, local_in, norm_attend)
    grad_local_norm, grad_norm_attend = pull_local(grad_attend_normed)
    grad_local = grad_after + grad_local_norm
    grad_slots_low = grad_local.astype(jnp.bfloat16).reshape(patches, PATCH * D)
    grad_patch_out = left_product(global_low, grad_slots_low)
    grad_global_out = right_product(grad_slots_low, w_patch_out)
    grad_mixer_low = grad_global_out.astype(jnp.bfloat16)
    grad_mixer_out = left_product(mixed_low, grad_mixer_low)
    grad_mixed = right_product(grad_mixer_low, w_mixer_out)
    _, pull_output = jax.vjp(
        mixer_output,
        heads_x,
        input_map,
        output_map,
        step_size,
        log_decay,
        carried,
        gate_part,
        skip_gain,
        norm_gated,
    )
    (
        grad_heads,
        grad_input_map,
        grad_output_map,
        grad_step,
        grad_log_decay,
        grad_carried,
        grad_gate_part,
        grad_skip_gain,
        grad_norm_gated,
    ) = pull_output(grad_mixed)
    _, later_grads = prefix((decay_all, grad_carried), "dp", combine_carry, identity)
    grad_decay_all = jnp.sum(carried * later_grads, axis=(1, 2))
    _, pull_state = jax.vjp(block_state, heads_x, input_map, step_size, log_decay)
    more_heads, more_input_map, more_step, more_log_decay = pull_state(
        (grad_decay_all, later_grads)
    )
    _, pull_inputs = jax.vjp(
        mixer_inputs, extended, step_raw, conv_weight, conv_bias, step_bias, decay_rate
    )
    (
        grad_extended,
        grad_step_raw,
        grad_conv_weight,
        grad_conv_bias,
        grad_step_bias,
        grad_decay_rate,
    ) = pull_inputs(
        (
            grad_heads + more_heads,
            grad_input_map + more_input_map,
            grad_output_map,
            grad_step + more_step,
            grad_log_decay + more_log_decay,
        )
    )
    returned = passed_along(grad_extended[: CONV - 1], "dp", -1)
    grad_conv_input = grad_extended[CONV - 1 :] + jnp.pad(
        returned, ((patches - (CONV - 1), 0), (0, 0))
    )
    grad_projected_low = jnp.concatenate(
        [grad_gate_part, grad_conv_input, grad_step_raw], axis=1
    ).astype(jnp.bfloat16)
    grad_mixer_in = left_product(normed_low, grad_projected_low)
    grad_normed = right_product(grad_projected_low, w_mixer_in)
    _, pull_global = jax.vjp(root_norm, global_in, norm_global)
    grad_global_norm, grad_norm_global = pull_global(grad_normed)
    grad_global_low = (grad_global_out + grad_global_norm).astype(jnp.bfloat16)
    grad_patch_in = left_product(patch_rows, grad_global_low)
    grad_patch_rows = right_product(grad_global_low, w_patch_in).reshape(rows, D)
    grad_bytes = ((grad_local + grad_patch_rows) * keep).astype(jnp.bfloat16)[None]
    flat_grads = (
        lax.psum_scatter(grad_patch_in.reshape(-1), ("dp", "mp"), scatter_dimension=0, tiled=True),
        lax.psum_scatter(grad_mixer_in.reshape(-1), ("dp", "mp"), scatter_dimension=0, tiled=True),
        lax.psum_scatter(grad_mixer_out.reshape(-1), ("dp", "mp"), scatter_dimension=0, tiled=True),
        lax.psum_scatter(grad_patch_out.reshape(-1), ("dp", "mp"), scatter_dimension=0, tiled=True),
        lax.psum_scatter(grad_attend_in.reshape(-1), ("dp", "mp"), scatter_dimension=0, tiled=True),
        lax.psum_scatter(
            grad_attend_out.reshape(-1), ("dp", "mp"), scatter_dimension=0, tiled=True
        ),
    )
    small = lax.psum(
        (
            grad_norm_global,
            grad_conv_weight,
            grad_conv_bias,
            grad_step_bias,
            grad_decay_rate,
            grad_skip_gain,
            grad_norm_gated,
            grad_norm_attend,
            grad_norm_feed,
        ),
        ("dp", "mp"),
    )
    return (
        out_bytes,
        grad_bytes,
        flat_grads[0],
        flat_grads[1],
        flat_grads[2],
        flat_grads[3],
        flat_grads[4],
        flat_grads[5],
        grad_gate,
        grad_up,
        grad_down,
        small[0],
        small[1],
        small[2],
        small[3],
        small[4],
        small[5],
        small[6],
        small[7],
        small[8],
    )


def solution(mesh):
    return jax.shard_map(
        body,
        mesh=mesh,
        in_specs=(
            P("mp", "dp", None),
            P(),
            P(("dp", "mp")),
            P(("dp", "mp")),
            P(("dp", "mp")),
            P(("dp", "mp")),
            P(("dp", "mp")),
            P(("dp", "mp")),
            P("dp", "mp"),
            P("dp", "mp"),
            P("mp", "dp"),
            P(),
            P(),
            P(),
            P(),
            P(),
            P(),
            P(),
            P(),
            P(),
            P("mp", "dp", None),
        ),
        out_specs=(
            P("mp", "dp", None),
            P("mp", "dp", None),
            P(("dp", "mp")),
            P(("dp", "mp")),
            P(("dp", "mp")),
            P(("dp", "mp")),
            P(("dp", "mp")),
            P(("dp", "mp")),
            P("dp", "mp"),
            P("dp", "mp"),
            P("mp", "dp"),
            P(),
            P(),
            P(),
            P(),
            P(),
            P(),
            P(),
            P(),
            P(),
        ),
        check_vma=False,
    )
```

profile of v0, /device:TPU:0, one launch (start us, length us, event | category | flops | bytes accessed | tf_op | source)
XLA Modules:
  0.0 3119.5 jit_solution(7548651199191854836)
XLA Ops:
  15.5 78.0 %all-gather.19.cloned.1.call-done = bf16[4489216]{0:T(1024)(128)(2,1)} async-done(((bf16[140288]{0:T(1024)(128)(2,1)}), bf16[4489216]{0:T(1024)(128)(2,1)}) %all-gather.19.cloned.1.call-update) | async-done | bytes 8978448 | tf_op jit(solution)/shard_map/all_gather | solution.py:165
  93.5 18.7 reshape.377
  112.2 97.6 %all-gather.17.cloned.1.call-done = bf16[8388608]{0:T(1024)(128)(2,1)} async-done(((bf16[262144]{0:T(1024)(128)(2,1)}), bf16[8388608]{0:T(1024)(128)(2,1)}) %all-gather.17.cloned.1.call-update) | async-done | bytes 16777232 | tf_op jit(solution)/shard_map/all_gather | solution.py:164
  209.8 25.3 reshape.376
  235.2 9.1 multiply_reduce_fusion.20
  271.5 59.4 %all-gather.21.cloned.1.call-done = bf16[2097152]{0:T(1024)(128)(2,1)} async-done(((bf16[65536]{0:T(1024)(128)(2,1)}), bf16[2097152]{0:T(1024)(128)(2,1)}) %all-gather.21.cloned.1.call-update) | async-done | bytes 4194320 | tf_op jit(solution)/shard_map/all_gather | solution.py:166
  338.2 63.5 %all-gather.25.cloned.1.call-done = bf16[3145728]{0:T(1024)(128)(2,1)} async-done(((bf16[98304]{0:T(1024)(128)(2,1)}), bf16[3145728]{0:T(1024)(128)(2,1)}) %all-gather.25.cloned.1.call-update) | async-done | bytes 6291472 | tf_op jit(solution)/shard_map/all_gather | solution.py:168
  401.8 10.3 reshape.383
  412.3 18.9 all-gather.2
  431.8 86.1 %all-gather.23.cloned.1.call-done = bf16[8388608]{0:T(1024)(128)(2,1)} async-done(((bf16[262144]{0:T(1024)(128)(2,1)}), bf16[8388608]{0:T(1024)(128)(2,1)}) %all-gather.23.cloned.1.call-update) | async-done | bytes 16777232 | tf_op jit(solution)/shard_map/all_gather | solution.py:167
  517.9 25.5 reshape.381
  544.4 47.8 %all-gather.39.cloned.1.call-done = bf16[256,64,128]{2,1,0:T(8,128)(2,1)} async-done(((bf16[32,64,128]{2,1,0:T(8,128)(2,1)}), bf16[256,64,128]{2,1,0:T(8,128)(2,1)}) %all-gather.39.cloned.1.call-update) | async-done | bytes 4194320 | tf_op jit(solution)/shard_map/all_gather | solution.py:31
  608.3 10.3 fusion.163
  649.6 13.7 fusion.17
  667.1 9.6 convert_bitcast_fusion
  687.0 44.4 %all-gather.29.cloned.1.call-done = bf16[2048,1024]{1,0:T(8,128)(2,1)} async-done(((bf16[512,1024]{1,0:T(8,128)(2,1)}), bf16[2048,1024]{1,0:T(8,128)(2,1)}) %all-gather.29.cloned.1.call-update) | async-done | bytes 4194320 | tf_op jit(solution)/shard_map/all_gather | solution.py:255
  731.4 10.7 fusion.166
  742.1 40.6 %all-gather.31.cloned.1.call-done = bf16[1024,1024]{1,0:T(8,128)(2,1)} async-done(((bf16[128,1024]{1,0:T(8,128)(2,1)}), bf16[1024,1024]{1,0:T(8,128)(2,1)}) %all-gather.31.cloned.1.call-update) | async-done | bytes 2097168 | tf_op jit(solution)/shard_map/all_gather | solution.py:217
  782.7 10.7 fusion.165
  793.4 40.9 %all-gather.35.cloned.1.call-done = bf16[1024,1024]{1,0:T(8,128)(2,1)} async-done(((bf16[1024,128]{1,0:T(8,128)(2,1)}), bf16[1024,1024]{1,0:T(8,128)(2,1)}) %all-gather.35.cloned.1.call-update) | async-done | bytes 2097168 | tf_op jit(solution)/shard_map/all_gather | solution.py:219
  834.3 34.7 %all-gather.37.cloned.1.call-done = bf16[2048,1024]{1,0:T(8,128)(2,1)} async-done(((bf16[512,1024]{1,0:T(8,128)(2,1)}), bf16[2048,1024]{1,0:T(8,128)(2,1)}) %all-gather.37.cloned.1.call-update) | async-done | bytes 4194320 | tf_op jit(solution)/shard_map/all_gather | solution.py:271
  869.0 16.1 multiply_convert_fusion
  892.3 8.6 add_convert_fusion
  901.0 9.7 convolution_convert_fusion
  916.0 29.6 reduce-scatter.10.cloned.1.call-done
  948.1 44.6 %reduce-scatter.8.cloned.1.call-done = bf16[512,1024]{1,0:T(8,128)(2,1)} async-done(((bf16[2048,1024]{1,0:T(8,128)(2,1)}), bf16[512,1024]{1,0:T(8,128)(2,1)}) %reduce-scatter.8.cloned.1.call-update) | async-done | bytes 1048592 | tf_op jit(solution)/shard_map/reduce_scatter | solution.py:261
  1002.2 9.5 fusion.26
  1011.8 17.5 convert_reduce_fusion
  1035.6 10.8 fusion.23
  1046.4 9.4 fusion.20
  1084.0 8.6 multiply_reduce_fusion.1
  1096.0 11.4 fusion.168
  1116.0 9.5 convolution_convert_fusion.1
  1129.8 9.4 convolution_convert_fusion.2
  1139.3 9.4 convolution_convert_fusion.3
  1168.7 13.5 convolution_bitcast_fusion.1
  1188.5 12.1 copy.281
  1200.5 8.8 copy.279
  1209.3 27.7 copy.280
  1238.5 16.3 while.29
  1287.0 8.2 fusion.103
  1295.2 23.0 reshape.397
  1325.6 13.4 convolution_bitcast_fusion
  1339.1 27.7 copy.278
  1370.9 28.6 reduce-scatter.12.cloned.1.call-done
  1403.3 12.3 fusion.169
  1420.2 1549.6 %all-reduce.29.cloned.1.call-done = (f32[8388608]{0:T(1024)}, f32[4489216]{0:T(1024)}, f32[2097152]{0:T(1024)}, f32[8388608]{0:T(1024)}, f32[3145728]{0:T(1024)}, /*index=5*/f32[1048576]{0:T(1024)}) async-done(((f32[8388608]{0:T(1024)}, f32[4489216]{0:T(1024)}, f32[2097152]{0:T(1024)}, f32[8388608]{0:T(1024)}, f32[3145728]{0:T(1024)}, /*index=5*/f32[1048576]{0:T(1024)}), (f32[8388608]{0:T(1024)}, ...) | async-done | bytes 110231568
  2981.2 119.6 %all-reduce.27.cloned.1.call-done = (f32[1024]{0:T(1024)}, f32[4,2304]{1,0:T(4,128)}, f32[2304]{0:T(1024)}, f32[32]{0:T(128)}, f32[32]{0:T(128)}, /*index=5*/f32...) async-done(((f32[1024]{0:T(1024)}, f32[4,2304]{1,0:T(4,128)}, f32[2304]{0:T(1024)}, f32[32]{0:T(128)}, f32[32]{0:T(128)}, /*index=5*/f32[32]{0:T(128)}, ...) | async-done | bytes 66960 | tf_op jit(solution)/shard_map/psum | solution.py:392
  (461 shorter events, 298.1 us)
Async XLA Ops:
  7.2 86.3 %all-gather.19.cloned.1.call-start = ((), (), s32[]{:S(2)}) async-start(), calls=%async_computation.6 | async-start | bytes 9259008 | tf_op jit(solution)/shard_map/all_gather | solution.py:165
  7.9 201.9 %all-gather.17.cloned.1.call-start = ((), (), s32[]{:S(2)}) async-start(), calls=%async_computation.5 | async-start | bytes 17301504 | tf_op jit(solution)/shard_map/all_gather | solution.py:164
  8.7 258.6 %all-gather.27.cloned.1.call-start = ((), (), s32[]{:S(2)}) async-start(), calls=%async_computation.10 | async-start | bytes 2162688 | tf_op jit(solution)/shard_map/all_gather | solution.py:169
  9.4 321.5 %all-gather.21.cloned.1.call-start = ((), (), s32[]{:S(2)}) async-start(), calls=%async_computation.7 | async-start | bytes 4325376 | tf_op jit(solution)/shard_map/all_gather | solution.py:166
  10.0 391.7 %all-gather.25.cloned.1.call-start = ((), (), s32[]{:S(2)}) async-start(), calls=%async_computation.9 | async-start | bytes 6488064 | tf_op jit(solution)/shard_map/all_gather | solution.py:168
  10.6 507.3 %all-gather.23.cloned.1.call-start = ((), (), s32[]{:S(2)}) async-start(), calls=%async_computation.8 | async-start | bytes 17301504 | tf_op jit(solution)/shard_map/all_gather | solution.py:167
  11.2 581.0 %all-gather.39.cloned.1.call-start = ((), (), s32[]{:S(2)}) async-start(), calls=%async_computation.20 | async-start | bytes 4718592 | tf_op jit(solution)/shard_map/all_gather | solution.py:31
  15.5 236.2 %copy-start.72 = (f32[2304]{0:T(1024)}, f32[2304]{0:T(1024)S(1)}, u32[]{:S(2)}) copy-start(f32[2304]{0:T(1024)S(1)} %get-tuple-element.233) | copy-start | bytes 27652
  15.5 236.2 %copy-start.74 = (f32[2304]{0:T(1024)}, f32[2304]{0:T(1024)S(1)}, u32[]{:S(2)}) copy-start(f32[2304]{0:T(1024)S(1)} %get-tuple-element.234) | copy-start | bytes 27652
  15.5 236.2 %copy-start.75 = (f32[2304]{0:T(1024)}, f32[2304]{0:T(1024)S(1)}, u32[]{:S(2)}) copy-start(f32[2304]{0:T(1024)S(1)} %get-tuple-element.235) | copy-start | bytes 27652
  15.5 236.2 %copy-start.76 = (f32[2304]{0:T(1024)}, f32[2304]{0:T(1024)S(1)}, u32[]{:S(2)}) copy-start(f32[2304]{0:T(1024)S(1)} %get-tuple-element.236) | copy-start | bytes 27652
  15.5 230.7 %copy-start.107 = (f32[32]{0:T(128)}, f32[32]{0:T(128)S(1)}, u32[]{:S(2)}) copy-start(f32[32]{0:T(128)S(1)} %exponential_negate_fusion) | copy-start | bytes 388
  244.3 359.5 %copy-start.19 = (f32[64,1024]{1,0:T(8,128)}, f32[64,1024]{1,0:T(8,128)S(1)}, u32[]{:S(2)}) copy-start(f32[64,1024]{1,0:T(8,128)S(1)} %get-tuple-element.311) | copy-start | bytes 786436
  246.6 165.5 %copy-start.52 = (f32[64,32]{0,1:T(8,128)}, f32[64,32]{0,1:T(8,128)S(1)}, u32[]{:S(2)}) copy-start(f32[64,32]{0,1:T(8,128)S(1)} %copy.219) | copy-start | bytes 24580
  246.6 5.0 collective-permute-start
  250.3 343.9 %copy-start.66 = (f32[64,32]{0,1:T(8,128)}, f32[64,32]{0,1:T(8,128)S(1)}, u32[]{:S(2)}) copy-start(f32[64,32]{0,1:T(8,128)S(1)} %get-tuple-element.308) | copy-start | bytes 24580
  250.4 343.9 %copy-start.68 = (f32[32,64]{1,0:T(8,128)}, f32[32,64]{1,0:T(8,128)S(1)}, u32[]{:S(2)}) copy-start(f32[32,64]{1,0:T(8,128)S(1)} %get-tuple-element.306) | copy-start | bytes 24580
  257.7 429.2 %all-gather.33.cloned.1.call-start = ((), (), s32[]{:S(2)}) async-start(), calls=%async_computation.13 | async-start | bytes 2359296 | tf_op jit(solution)/shard_map/all_gather | solution.py:218
  258.5 472.9 %all-gather.29.cloned.1.call-start = ((), (), s32[]{:S(2)}) async-start(), calls=%async_computation.11 | async-start | bytes 5242880 | tf_op jit(solution)/shard_map/all_gather | solution.py:255
  262.6 365.3 %copy-start.8 = (f32[64,8192]{1,0:T(8,128)}, f32[64,8192]{1,0:T(8,128)S(1)}, u32[]{:S(2)}) copy-start(f32[64,8192]{1,0:T(8,128)S(1)} %reshape.412) | copy-start | bytes 6291460
  431.8 162.4 %copy-start.56 = (f32[32,64]{1,0:T(8,128)}, f32[32,64]{1,0:T(8,128)S(1)}, u32[]{:S(2)}) copy-start(f32[32,64]{1,0:T(8,128)S(1)} %copy.216) | copy-start | bytes 24580
  544.3 49.9 %copy-start.60 = (f32[64,64]{1,0:T(8,128)}, f32[64,64]{1,0:T(8,128)S(1)}, u32[]{:S(2)}) copy-start(f32[64,64]{1,0:T(8,128)S(1)} %fusion.118) | copy-start | bytes 49156
  603.7 14.8 copy-start.112
  603.7 14.8 copy-start.100
  684.8 97.9 %all-gather.31.cloned.1.call-start = ((), (), s32[]{:S(2)}) async-start(), calls=%async_computation.12 | async-start | bytes 2359296 | tf_op jit(solution)/shard_map/all_gather | solution.py:217
  685.4 149.0 %all-gather.35.cloned.1.call-start = ((), (), s32[]{:S(2)}) async-start(), calls=%async_computation.14 | async-start | bytes 2359296 | tf_op jit(solution)/shard_map/all_gather | solution.py:219
  686.1 182.9 %all-gather.37.cloned.1.call-start = ((), (), s32[]{:S(2)}) async-start(), calls=%async_computation.16 | async-start | bytes 5242880 | tf_op jit(solution)/shard_map/all_gather | solution.py:271
  686.7 258.9 %reduce-scatter.10.cloned.1.call-start = ((), (), s32[]{:S(2)}) async-start(), calls=%async_computation.17 | async-start | bytes 5242880 | tf_op jit(solution)/shard_map/reduce_scatter | solution.py:280
  869.0 16.1 copy-start.115
  900.9 91.7 %reduce-scatter.8.cloned.1.call-start = ((), (), s32[]{:S(2)}) async-start(), calls=%async_computation.15 | async-start | bytes 5242880 | tf_op jit(solution)/shard_map/reduce_scatter | solution.py:261
  910.7 327.9 %all-gather.41.cloned.1.call-start = ((), (), s32[]{:S(2)}) async-start(), calls=%async_computation.21 | async-start | bytes 4718592 | tf_op jit(solution)/shard_map/all_gather | solution.py:51
  1115.9 251.2 %reduce-scatter.16.cloned.1.call-start = ((), (), s32[]{:S(2)}) async-start(), calls=%async_computation.22 | async-start | bytes 2359296
  1129.5 239.6 %reduce-scatter.14.cloned.1.call-start = ((), (), s32[]{:S(2)}) async-start(), calls=%async_computation.19 | async-start | bytes 2359296 | tf_op jit(solution)/shard_map/reduce_scatter | solution.py:292
  1139.2 260.3 %reduce-scatter.12.cloned.1.call-start = ((), (), s32[]{:S(2)}) async-start(), calls=%async_computation.18 | async-start | bytes 2359296 | tf_op jit(solution)/shard_map/reduce_scatter | solution.py:289
  1148.7 1821.2 %all-reduce.29.cloned.1.call-start = ((), (), s32[]{:S(2)}) async-start(), calls=%async_computation.24 | async-start | bytes 220463104
  1168.6 13.6 copy-start.57
  1168.7 13.6 copy-start.61
  1168.7 13.6 copy-start.69
  1168.7 13.6 copy-start.78
  1185.3 51.7 %copy-start.71 = (f32[64,64]{1,0:T(8,128)}, f32[64,64]{1,0:T(8,128)S(1)}, u32[]{:S(2)}) copy-start(f32[64,64]{1,0:T(8,128)S(1)} %get-tuple-element.226) | copy-start | bytes 49156
  1238.5 17.2 copy-start.65
  1279.7 6.1 collective-permute-start.1
  1366.7 34.6 %copy-start.86 = (f32[2048]{0:T(1024)S(1)}, f32[2048]{0:T(1024)}, u32[]{:S(2)}) copy-start(f32[2048]{0:T(1024)} %get-tuple-element.272) | copy-start | bytes 24580
  1366.7 35.3 %copy-start.82 = (f32[2304]{0:T(1024)S(1)}, f32[2304]{0:T(1024)}, u32[]{:S(2)}) copy-start(f32[2304]{0:T(1024)} %get-tuple-element.220) | copy-start | bytes 27652
  1366.7 35.3 %copy-start.81 = (f32[2304]{0:T(1024)S(1)}, f32[2304]{0:T(1024)}, u32[]{:S(2)}) copy-start(f32[2304]{0:T(1024)} %get-tuple-element.221) | copy-start | bytes 27652
  1366.7 35.3 %copy-start.80 = (f32[2304]{0:T(1024)S(1)}, f32[2304]{0:T(1024)}, u32[]{:S(2)}) copy-start(f32[2304]{0:T(1024)} %get-tuple-element.222) | copy-start | bytes 27652
  1366.7 35.4 %copy-start.117 = (f32[32]{0:T(128)S(1)}, f32[32]{0:T(128)}, u32[]{:S(2)}) copy-start(f32[32]{0:T(128)} %param.40) | copy-start | bytes 388
  1366.8 1734.1 %all-reduce.27.cloned.1.call-start = ((), (), s32[]{:S(2)}) async-start(), calls=%async_computation.23 | async-start | bytes 142336 | tf_op jit(solution)/shard_map/psum | solution.py:392
  (94 other events, 574.0 us)
Sparse Core Ops, SparseCore 0:
  11.0 82.4 all-gather.18
  96.3 113.4 all-gather.16
  212.7 54.5 all-gather.26
  270.0 60.8 all-gather.20
  333.7 68.0 all-gather.24
  404.5 113.3 all-gather.22
  520.6 71.5 all-gather.38
  594.3 47.5 all-gather.32
  684.9 46.4 all-gather.28
  733.4 49.2 all-gather.30
  784.8 49.5 all-gather.34
  836.3 32.6 all-gather.36
  901.0 44.4 reduce-scatter.9
  948.1 44.5 reduce-scatter.7
  1116.0 73.3 all-gather.40
  1192.9 66.1 reduce-scatter.15
  1262.4 66.7 reduce-scatter.13
  1332.6 66.8 reduce-scatter.11
  1405.9 1563.8 all-reduce.28
  2978.4 122.4 all-reduce.26
where the time goes:
time: 3130 us; the launch traced here: 3120 us
  waiting for transfers between devices  2380 us (76%)
  matrix products  318 us (10%)
  local copies, waits for them, and re-layouts  310 us (10%)
  other arithmetic  71.5 us (2%)
    unnamed x22, waiting for transfers between devices  1560 us
    unnamed x269, local copies, waits for them, and re-layouts  124 us
    psum x1, waiting for transfers between devices, body(): lax.psum((grad_norm_global, grad_conv_weight, grad_conv_bias, grad_step_b...  120 us
    all_gather x1, waiting for transfers between devices, fetch_weights(): lax.all_gather(patch_in, ('dp', 'mp'), axis=0, tiled=True)  97.6 us
    all_gather x1, waiting for transfers between devices, fetch_weights(): lax.all_gather(patch_out, ('dp', 'mp'), axis=0, tiled=True)  86.1 us
    all_gather x1, waiting for transfers between devices, fetch_weights(): lax.all_gather(mixer_in, ('dp', 'mp'), axis=0, tiled=True)  78 us
    dot_general x9, matrix products, left_product(): lax.dot_general(left, right, (((0,), (0,)), ((), ())), preferred_element_...  76.4 us
    dot_general x9, matrix products, right_product(): lax.dot_general(left, right, (((1,), (1,)), ((), ())), preferred_element_...  75.8 us
  transfers between devices with their start and end apart: 22, of which 18 were waited for; matrix products, arithmetic and copies ran while one was open for 17% of the time, Pallas kernels for 0%

commit v1 on v0

v1 whole, which is shorter than its diff:
```python
import functools

import jax
import jax.numpy as jnp
from jax import lax
from jax.experimental import pallas as pl
from jax.experimental.pallas import tpu as pltpu
from jax.sharding import PartitionSpec as P

D = 1024
PATCH = 8
INNER = 2048
HEADS_M = 32
STATE = 128
CONV = 4
HEADS_A = 16
HEAD_M = 64
HEAD_A = 64
PROJ = 4384
LANE = 128

HIGH = lax.Precision.HIGHEST
EPSILON = 1e-05
BF = jnp.bfloat16
F32 = jnp.float32


def exchange_kernel(plan, sizes, *refs):
    count = len(plan)
    sources, targets = refs[:count], refs[count : 2 * count]
    sems = refs[2 * count :]
    local_sem = sems[0]
    axes = sorted({axis for _, axis in plan})
    me = {axis: lax.axis_index(axis) for axis in axes}
    barrier = pltpu.get_barrier_semaphore()
    total = 0
    for axis in axes:
        for k in range(1, sizes[axis]):
            pl.semaphore_signal(
                barrier,
                inc=1,
                device_id={axis: lax.rem(me[axis] + k, sizes[axis])},
                device_id_type=pl.DeviceIdType.MESH,
            )
        total += sizes[axis] - 1
    pl.semaphore_wait(barrier, total)
    copies = []
    for index, (kind, axis) in enumerate(plan):
        send, recv = sems[1 + 2 * index], sems[2 + 2 * index]
        for k in range(1, sizes[axis]):
            peer = lax.rem(me[axis] + k, sizes[axis])
            source = sources[index].at[peer] if kind == "a2a" else sources[index]
            copy = pltpu.make_async_remote_copy(
                src_ref=source,
                dst_ref=targets[index].at[me[axis]],
                send_sem=send.at[k - 1],
                recv_sem=recv.at[k - 1],
                device_id={axis: peer},
                device_id_type=pl.DeviceIdType.MESH,
            )
            copy.start()
            copies.append(copy)
    own = []
    for index, (kind, axis) in enumerate(plan):
        source = sources[index].at[me[axis]] if kind == "a2a" else sources[index]
        copy = pltpu.make_async_copy(source, targets[index].at[me[axis]], local_sem.at[index])
        copy.start()
        own.append(copy)
    for copy in own:
        copy.wait()
    for copy in copies:
        copy.wait()


def exchange(ident, *steps):
    plan = tuple((kind, axis) for kind, axis, _ in steps)
    arrays = [array for _, _, array in steps]
    sizes = {axis: lax.axis_size(axis) for _, axis in plan}
    shapes = [
        jax.ShapeDtypeStruct(
            array.shape if kind == "a2a" else (sizes[axis],) + array.shape, array.dtype
        )
        for kind, axis, array in steps
    ]
    scratch = [pltpu.SemaphoreType.DMA((len(plan),))]
    for _, axis in plan:
        scratch += [pltpu.SemaphoreType.DMA((sizes[axis] - 1,))] * 2
    return pl.pallas_call(
        functools.partial(exchange_kernel, plan, sizes),
        out_shape=shapes,
        in_specs=[pl.BlockSpec(memory_space=pl.ANY)] * len(plan),
        out_specs=[pl.BlockSpec(memory_space=pl.ANY)] * len(plan),
        scratch_shapes=scratch,
        compiler_params=pltpu.CompilerParams(collective_id=ident, has_side_effects=True),
    )(*arrays)


def product(left, right):
    return jnp.dot(left, right, preferred_element_type=F32)


def left_product(left, right):
    return lax.dot_general(left, right, (((0,), (0,)), ((), ())), preferred_element_type=F32)


def right_product(left, right):
    return lax.dot_general(left, right, (((1,), (1,)), ((), ())), preferred_element_type=F32)


def total(parts):
    return jnp.sum(parts.astype(F32), axis=0)


def root_norm(values, gain):
    return values * lax.rsqrt(jnp.mean(values * values, axis=-1, keepdims=True) + EPSILON) * gain


def convolve(extended, conv_weight, conv_bias):
    count = extended.shape[0] - (CONV - 1)
    summed = conv_bias + conv_weight[0] * extended[0:count]
    for shift in range(1, CONV):
        summed = summed + conv_weight[shift] * extended[shift : shift + count]
    return jax.nn.silu(summed)


def gated_heads(gate_part, conv_input, step_raw, conv_weight, conv_bias, step_bias, decay_rate, skip_gain):
    count, heads = step_raw.shape
    inner = heads * HEAD_M
    extended = jnp.concatenate([jnp.zeros((CONV - 1, conv_input.shape[1]), F32), conv_input], axis=0)
    activated = convolve(extended, conv_weight, conv_bias)
    heads_x = activated[:, :inner].reshape(count, heads, HEAD_M)
    input_map = activated[:, inner : inner + STATE]
    output_map = activated[:, inner + STATE :]
    step_size = jax.nn.softplus(step_raw + step_bias)
    log_decay = jnp.cumsum(step_size * -jnp.exp(decay_rate), axis=0)
    decay_t = log_decay.T
    spread = decay_t[:, :, None] - decay_t[:, None, :]
    causal = jnp.arange(count)[:, None] >= jnp.arange(count)[None, :]
    factor = jnp.exp(jnp.where(causal[None], spread, -jnp.inf))
    scores = jnp.dot(output_map, input_map.T, precision=HIGH)
    weights = factor * scores[None] * step_size.T[:, None, :]
    values = jnp.einsum("hts,shp->thp", weights, heads_x, precision=HIGH)
    values = values + skip_gain[None, :, None] * heads_x
    return values.reshape(count, inner) * jax.nn.silu(gate_part)


def patch_attention(attend_proj):
    count = attend_proj.shape[0]
    patches = count // PATCH
    query = attend_proj[:, :D].reshape(patches, PATCH, HEADS_A, HEAD_A)
    keyed = attend_proj[:, D : 2 * D].reshape(patches, PATCH, HEADS_A, HEAD_A)
    valued = attend_proj[:, 2 * D :].reshape(patches, PATCH, HEADS_A, HEAD_A)
    scores = jnp.einsum("pihd,pjhd->phij", query, keyed, precision=HIGH) * HEAD_A ** (-0.5)
    causal = jnp.arange(PATCH)[:, None] >= jnp.arange(PATCH)[None, :]
    scores = jnp.where(causal, scores, -jnp.inf)
    top = jnp.max(scores, axis=-1, keepdims=True)
    expo = jnp.exp(scores - top)
    probs = expo / jnp.sum(expo, axis=-1, keepdims=True)
    result = jnp.einsum("phij,pjhd->pihd", probs, valued, precision=HIGH)
    return result.reshape(count, D)


def own_columns(array, place, width):
    return lax.dynamic_slice_in_dim(array, place * width, width, axis=-1)


def tucked(row):
    return jnp.pad(row[:, None, :], ((0, 0), (0, 7), (0, -row.shape[1] % LANE)))


def body(
    byte_embeds,
    lengths,
    patch_in,
    mixer_in,
    mixer_out,
    patch_out,
    attend_in,
    attend_out,
    gate_weight,
    up_weight,
    down_weight,
    norm_global,
    conv_weight,
    conv_bias,
    step_bias,
    decay_rate,
    skip_gain,
    norm_gated,
    norm_attend,
    norm_feed,
    cotangent,
):
    n_dp, n_mp = lax.axis_size("dp"), lax.axis_size("mp")
    devices = n_dp * n_mp
    rows = byte_embeds.shape[1]
    patches = rows // PATCH
    count = patches * n_dp
    group = lax.axis_index("mp")
    place = lax.axis_index("dp")
    length = jnp.sum(jnp.where(jnp.arange(lengths.shape[0], dtype=jnp.int32) == group, lengths, 0))
    position = place * rows + jnp.arange(rows, dtype=jnp.int32)
    keep = (position < length).astype(F32)[:, None]
    inputs = byte_embeds[0].astype(F32) * keep

    heads = HEADS_M // n_dp
    inner = heads * HEAD_M
    byte_cols = PATCH * D // n_dp
    k_rows = D // devices
    step_pad = -heads % LANE
    cols = 2 * inner + 2 * STATE + heads + step_pad

    w_attend = lax.all_gather(attend_in, ("dp", "mp"), axis=0, tiled=True).reshape(D, 3 * D)
    w_attend_out = lax.all_gather(attend_out, ("dp", "mp"), axis=0, tiled=True).reshape(D, D)
    w_gate, w_up, w_down = (
        lax.all_gather(gate_weight, "dp", axis=0, tiled=True),
        lax.all_gather(up_weight, "dp", axis=0, tiled=True),
        lax.all_gather(down_weight, "dp", axis=1, tiled=True),
    )
    grad_final = cotangent[0].astype(F32) * keep
    grad_feed_rows = lax.all_gather(grad_final.astype(BF), "mp", axis=0, tiled=True)

    mixer_rows = mixer_in.reshape(k_rows, PROJ)
    shared = mixer_rows[:, 2 * INNER : 2 * INNER + 2 * STATE]
    by_part = jnp.concatenate(
        [
            mixer_rows[:, :INNER].reshape(k_rows, n_dp, inner),
            mixer_rows[:, INNER : 2 * INNER].reshape(k_rows, n_dp, inner),
            jnp.broadcast_to(shared[:, None], (k_rows, n_dp, 2 * STATE)),
            mixer_rows[:, 2 * INNER + 2 * STATE :].reshape(k_rows, n_dp, heads),
            jnp.zeros((k_rows, n_dp, step_pad), BF),
        ],
        axis=2,
    ).transpose(1, 0, 2)
    out_by_part = patch_out.reshape(k_rows, n_dp, byte_cols).transpose(1, 0, 2)
    patch_rows = inputs.astype(BF).reshape(patches, n_dp, byte_cols).transpose(1, 0, 2)
    patch_rows, mixer_cols, out_cols, w_patch_in, w_mixer_out = exchange(
        0,
        ("a2a", "dp", patch_rows),
        ("a2a", "dp", by_part),
        ("a2a", "dp", out_by_part),
        ("ag", "mp", patch_in.reshape(-1, D)),
        ("ag", "mp", mixer_out.reshape(-1, D)),
    )
    patch_rows = patch_rows.reshape(count, byte_cols)
    w_patch_in = w_patch_in.reshape(byte_cols, D)
    w_mixer_out = w_mixer_out.reshape(inner, D)
    parts = product(patch_rows, w_patch_in).astype(BF).reshape(n_dp, patches, D)
    parts, mixer_cols, out_cols = exchange(
        1, ("a2a", "dp", parts), ("ag", "mp", mixer_cols), ("ag", "mp", out_cols)
    )
    w_mixer_in = mixer_cols.transpose(1, 0, 2, 3).reshape(D, cols)
    w_patch_out = out_cols.transpose(1, 0, 2, 3).reshape(D, byte_cols)
    global_in = total(parts)
    (normed,) = exchange(2, ("ag", "dp", root_norm(global_in, norm_global).astype(BF)))
    normed = normed.reshape(count, D)
    projected = product(normed, w_mixer_in)

    def own_conv(array):
        return jnp.concatenate(
            [own_columns(array[..., :INNER], place, inner), array[..., INNER:]], axis=-1
        )

    gated, pull_heads = jax.vjp(
        gated_heads,
        projected[:, :inner],
        projected[:, inner : 2 * inner + 2 * STATE],
        projected[:, 2 * inner + 2 * STATE : 2 * inner + 2 * STATE + heads],
        own_conv(conv_weight),
        own_conv(conv_bias),
        own_columns(step_bias, place, heads),
        own_columns(decay_rate, place, heads),
        own_columns(skip_gain, place, heads),
    )
    own_gain = own_columns(norm_gated, place, inner)
    squares = jnp.sum(gated * gated, axis=1).reshape(n_dp, patches)
    parts = product((gated * own_gain).astype(BF), w_mixer_out).astype(BF)
    parts, squares = exchange(
        3, ("a2a", "dp", parts.reshape(n_dp, patches, D)), ("a2a", "dp", tucked(squares))
    )
    scale = lax.rsqrt(total(squares)[0, :patches] / INNER + EPSILON)
    unscaled = total(parts)
    global_out = global_in + scale[:, None] * unscaled
    global_low, scales = exchange(
        4, ("ag", "dp", global_out.astype(BF)), ("ag", "dp", tucked(scale[None])[0])
    )
    global_low = global_low.reshape(count, D)
    scales = scales[:, 0, :patches].reshape(count, 1)
    slots = product(global_low, w_patch_out).astype(BF)
    (slots,) = exchange(5, ("a2a", "dp", slots.reshape(n_dp, patches, byte_cols)))
    local_in = inputs + slots.astype(F32).transpose(1, 0, 2).reshape(rows, D)

    attend_low = root_norm(local_in, norm_attend).astype(BF)
    attend_proj = product(attend_low, w_attend)
    attended_low = patch_attention(attend_proj).astype(BF)
    after_attend = local_in + product(attended_low, w_attend_out)
    feed_low = root_norm(after_attend, norm_feed).astype(BF)
    feed_rows = lax.all_gather(feed_low, "mp", axis=0, tiled=True)
    gate_value = product(feed_rows, w_gate)
    up_value = product(feed_rows, w_up)
    sigmoid_gate = jax.nn.sigmoid(gate_value)
    silu_gate = gate_value * sigmoid_gate
    hidden_low = (silu_gate * up_value).astype(BF)
    feed_out = lax.psum_scatter(
        product(hidden_low, w_down).astype(BF), "mp", scatter_dimension=0, tiled=True
    ).astype(F32)
    out_bytes = ((after_attend + feed_out) * keep).astype(BF)[None]

    grad_hidden = right_product(grad_feed_rows, w_down)
    grad_down = left_product(hidden_low, grad_feed_rows)
    grad_gate_low = (
        grad_hidden * up_value * sigmoid_gate * (1.0 + gate_value * (1.0 - sigmoid_gate))
    ).astype(BF)
    grad_up_low = (grad_hidden * silu_gate).astype(BF)
    grad_gate = left_product(feed_rows, grad_gate_low)
    grad_up = left_product(feed_rows, grad_up_low)
    grad_feed_normed = lax.psum_scatter(
        (right_product(grad_gate_low, w_gate) + right_product(grad_up_low, w_up)).astype(BF),
        "mp",
        scatter_dimension=0,
        tiled=True,
    ).astype(F32)
    grad_gate, grad_up, grad_down = (
        lax.psum_scatter(grad_gate.astype(BF), "dp", scatter_dimension=0, tiled=True).astype(F32),
        lax.psum_scatter(grad_up.astype(BF), "dp", scatter_dimension=0, tiled=True).astype(F32),
        lax.psum_scatter(grad_down.astype(BF), "dp", scatter_dimension=1, tiled=True).astype(F32),
    )
    _, pull_feed = jax.vjp(root_norm, after_attend, norm_feed)
    grad_after_norm, grad_norm_feed = pull_feed(grad_feed_normed)
    grad_after = grad_final + grad_after_norm
    grad_attend_low = grad_after.astype(BF)
    grad_attend_out = left_product(attended_low, grad_attend_low)
    grad_attended = right_product(grad_attend_low, w_attend_out)
    _, pull_attend = jax.vjp(patch_attention, attend_proj)
    (grad_proj,) = pull_attend(grad_attended)
    grad_proj_low = grad_proj.astype(BF)
    grad_attend_in = left_product(attend_low, grad_proj_low)
    grad_attend_normed = right_product(grad_proj_low, w_attend)
    _, pull_local = jax.vjp(root_norm, local_in, norm_attend)
    grad_local_norm, grad_norm_attend = pull_local(grad_attend_normed)
    grad_local = grad_after + grad_local_norm

    def owners(grad):
        split = grad.reshape(n_dp, n_mp, -1, grad.shape[-1])
        return split.transpose(1, 0, 2, 3).astype(BF)

    grad_slots = grad_local.astype(BF).reshape(patches, n_dp, byte_cols).transpose(1, 0, 2)
    grad_attend = owners(jnp.concatenate([grad_attend_in, grad_attend_out], axis=1))
    grad_slots, grad_attend = exchange(
        6, ("a2a", "dp", grad_slots), ("a2a", "mp", grad_attend)
    )
    grad_slots = grad_slots.reshape(count, byte_cols)
    grad_patch_out = owners(left_product(global_low, grad_slots))
    parts = right_product(grad_slots, w_patch_out).astype(BF).reshape(n_dp, patches, D)
    parts, grad_attend, grad_patch_out = exchange(
        7,
        ("a2a", "dp", parts),
        ("a2a", "dp", total(grad_attend).astype(BF)),
        ("a2a", "mp", grad_patch_out),
    )
    grad_attend = total(grad_attend)
    grad_global_out = total(parts)
    grad_mixer_low = grad_global_out.astype(BF)
    along = jnp.sum(grad_mixer_low.astype(F32) * unscaled, axis=1)
    grad_mixer_low, alongs, grad_patch_out = exchange(
        8,
        ("ag", "dp", grad_mixer_low),
        ("ag", "dp", tucked(along[None])[0]),
        ("a2a", "dp", total(grad_patch_out).astype(BF)),
    )
    grad_patch_out = grad_patch_out.astype(F32).transpose(1, 0, 2).reshape(-1)
    grad_mixer_low = grad_mixer_low.reshape(count, D)
    alongs = alongs[:, 0, :patches].reshape(count, 1)
    grad_mixer_out = left_product((gated * scales * own_gain).astype(BF), grad_mixer_low).astype(BF)
    grad_mixed = right_product(grad_mixer_low, w_mixer_out)
    grad_norm_gated = jnp.sum(grad_mixed * gated * scales, axis=0)
    grad_gated = scales * own_gain * grad_mixed - gated * (scales**3 * alongs / INNER)
    (
        grad_gate_part,
        grad_conv_input,
        grad_step_raw,
        grad_conv_weight,
        grad_conv_bias,
        grad_step_bias,
        grad_decay_rate,
        grad_skip_gain,
    ) = pull_heads(grad_gated)
    grad_projected = jnp.concatenate(
        [
            grad_gate_part,
            grad_conv_input,
            grad_step_raw,
            jnp.zeros((count, step_pad), F32),
        ],
        axis=1,
    ).astype(BF)
    parts = right_product(grad_projected, w_mixer_in).astype(BF).reshape(n_dp, patches, D)
    grad_mixer_in = owners(left_product(normed, grad_projected))
    parts, grad_mixer_out, grad_mixer_in = exchange(
        9,
        ("a2a", "dp", parts),
        ("a2a", "mp", grad_mixer_out.reshape(n_mp, -1, D)),
        ("a2a", "mp", grad_mixer_in),
    )
    grad_mixer_out = total(grad_mixer_out).reshape(-1)
    _, pull_global = jax.vjp(root_norm, global_in, norm_global)
    grad_global_norm, grad_norm_global = pull_global(total(parts))
    grad_global_low = (grad_global_out + grad_global_norm).astype(BF)

    def all_columns(part, whole):
        return lax.dynamic_update_slice_in_dim(
            jnp.zeros(part.shape[:-1] + (whole,), F32), part, place * part.shape[-1], axis=-1
        )

    small = [
        grad_norm_global,
        jnp.concatenate(
            [all_columns(grad_conv_weight[:, :inner], INNER), grad_conv_weight[:, inner:]], axis=1
        ),
        jnp.concatenate([all_columns(grad_conv_bias[:inner], INNER), grad_conv_bias[inner:]]),
        all_columns(grad_step_bias, HEADS_M),
        all_columns(grad_decay_rate, HEADS_M),
        all_columns(grad_skip_gain, HEADS_M),
        all_columns(grad_norm_gated, INNER),
        grad_norm_attend,
        grad_norm_feed,
    ]
    packed = jnp.concatenate([part.reshape(-1) for part in small])
    packed = jnp.pad(packed, (0, -packed.shape[0] % (8 * LANE))).reshape(-1, LANE)
    grad_global_low, packed, grad_mixer_in = exchange(
        10,
        ("ag", "dp", grad_global_low),
        ("ag", "mp", packed),
        ("a2a", "dp", total(grad_mixer_in).astype(BF)),
    )
    grad_global_low = grad_global_low.reshape(count, D)
    grad_patch_rows = right_product(grad_global_low, w_patch_in).astype(BF)
    grad_patch_in = left_product(patch_rows, grad_global_low).astype(BF)
    grad_patch_rows, grad_patch_in, packed = exchange(
        11,
        ("a2a", "dp", grad_patch_rows.reshape(n_dp, patches, byte_cols)),
        ("a2a", "mp", grad_patch_in.reshape(n_mp, -1, D)),
        ("ag", "dp", total(packed)),
    )
    grad_patch_in = total(grad_patch_in).reshape(-1)
    grad_patch_rows = grad_patch_rows.astype(F32).transpose(1, 0, 2).reshape(rows, D)
    grad_bytes = ((grad_local + grad_patch_rows) * keep).astype(BF)[None]
    grad_mixer_in = grad_mixer_in.astype(F32).transpose(1, 0, 2)
    edges = (inner, 2 * inner, 2 * inner + 2 * STATE, 2 * inner + 2 * STATE + heads)
    grad_mixer_in = jnp.concatenate(
        [
            grad_mixer_in[:, :, : edges[0]].reshape(k_rows, INNER),
            grad_mixer_in[:, :, edges[0] : edges[1]].reshape(k_rows, INNER),
            jnp.sum(grad_mixer_in[:, :, edges[1] : edges[2]], axis=1),
            grad_mixer_in[:, :, edges[2] : edges[3]].reshape(k_rows, HEADS_M),
        ],
        axis=1,
    ).reshape(-1)
    packed = total(packed).reshape(-1)
    summed, start = [], 0
    for part in small:
        summed.append(packed[start : start + part.size].reshape(part.shape))
        start += part.size
    return (
        out_bytes,
        grad_bytes,
        grad_patch_in,
        grad_mixer_in,
        grad_mixer_out,
        grad_patch_out,
        grad_attend[:, : 3 * D].reshape(-1),
        grad_attend[:, 3 * D :].reshape(-1),
        grad_gate,
        grad_up,
        grad_down,
        *summed,
    )


def solution(mesh):
    flat = P(("dp", "mp"))
    split = P("mp", "dp", None)
    return jax.shard_map(
        body,
        mesh=mesh,
        in_specs=(split, P())
        + (flat,) * 6
        + (P("dp", "mp"), P("dp", "mp"), P("mp", "dp"))
        + (P(),) * 9
        + (split,),
        out_specs=(split, split)
        + (flat,) * 6
        + (P("dp", "mp"), P("dp", "mp"), P("mp", "dp"))
        + (P(),) * 9,
        check_vma=False,
    )
```

time: 3130 us -> 1460 us (0.47)
  waiting for transfers between devices: 2380 us -> 399 us
  Pallas kernels: 0 us -> 549 us
  local copies, waits for them, and re-layouts: 310 us -> 135 us
  matrix products: 318 us -> 249 us
    unnamed x22 -> x13, waiting for transfers between devices: 1560 us -> 18.1 us
    pallas_call x0 -> x12, Pallas kernels: none -> 549 us  [exchange(): pl.pallas_call(functools.partial(exchange_kernel, plan, sizes), out_shape...]
    all_gather x9 -> x3, waiting for transfers between devices: 469 us -> 34.8 us  [the longest x1 34.8 us: body(): lax.all_gather(grad_final.astype(BF), 'mp', axis=0, tiled=True)]
    psum x1 -> x0, waiting for transfers between devices: 120 us -> none  [body(): lax.psum((grad_norm_global, grad_conv_weight, grad_conv_bias, grad_step_b...]
    reduce_scatter x3, waiting for transfers between devices: 73.2 us -> 182 us  [the longest x1 68.2 us: body(): lax.psum_scatter(grad_up.astype(BF), 'dp', scatter_dimension=0, tiled=True)]
    unnamed x269 -> x198, local copies, waits for them, and re-layouts: 124 us -> 19.2 us
    reshape x21, local copies, waits for them, and re-layouts: 128 us -> 31.1 us  [the longest x1 10.3 us: body(): lax.all_gather(attend_in, ('dp', 'mp'), axis=0, tiled=True)]
    all_gather x1, waiting for transfers between devices: 0.02 us -> 40.7 us  [body(): lax.all_gather(up_weight, 'dp', axis=0, tiled=True)]
  transfers between devices with their start and end apart: 22 -> 12, of which waited for: 18 -> 9; matrix products, arithmetic and copies ran while one was open for 17% -> 15% of each run, Pallas kernels for 0% -> 17%
where the time goes in v1:
time: 1460 us; the launch traced here: 1450 us
  Pallas kernels  549 us (38%)
  waiting for transfers between devices  399 us (27%)
  matrix products  249 us (17%)
  local copies, waits for them, and re-layouts  135 us (9%)
  other arithmetic  102 us (7%)
  between operations  16.1 us (1%)
    pallas_call x12, Pallas kernels, exchange(): pl.pallas_call(functools.partial(exchange_kernel, plan, sizes), out_shape...  549 us
    reduce_scatter x1, waiting for transfers between devices, body(): lax.psum_scatter(grad_up.astype(BF), 'dp', scatter_dimension=0, tiled=True)  68.2 us
    reduce_scatter x1, waiting for transfers between devices, body(): lax.psum_scatter(grad_gate.astype(BF), 'dp', scatter_dimension=0, tiled=T...  68.2 us
    dot_general x9, matrix products, product(): return jnp.dot(left, right, preferred_element_type=F32)  53.9 us
    dot_general x9, matrix products, right_product(): lax.dot_general(left, right, (((1,), (1,)), ((), ())), preferred_element_...  51.1 us
    dot_general x9, matrix products, left_product(): lax.dot_general(left, right, (((0,), (0,)), ((), ())), preferred_element_...  49.2 us
    reduce_scatter x1, waiting for transfers between devices, body(): lax.psum_scatter(product(hidden_low, w_down).astype(BF), 'mp', scatter_di...  45.2 us
    reduce_scatter x1, waiting for transfers between devices, body(): lax.psum_scatter((right_product(grad_gate_low, w_gate) + right_product(gr...  44.2 us
  transfers between devices with their start and end apart: 12, of which 9 were waited for; matrix products, arithmetic and copies ran while one was open for 15% of the time, Pallas kernels for 17%

profile of v1, /device:TPU:0, one launch (start us, length us, event | category | flops | bytes accessed | tf_op | source)
XLA Modules:
  0.0 1450.7 jit_solution(5310349384832232003)
XLA Ops:
  22.1 51.9 %shard_map.356 = (bf16[8,64,1024]{2,1,0:T(8,128)(2,1)}, bf16[8,32,896]{2,1,0:T(8,128)(2,1)}, bf16[8,32,1024]{2,1,0:T(8,128)(2,1)}, bf16[4,256,1024]{2,1,0:T(8,128)(2,1)}, bf16[4,64,1024]{2,1,0:T(8,128)(2,1)}) custom-call(bf16[8,64,1024]{2,1,0:T(8,128)(2,1)} %fusion.83.refs_0_, bf16[8,32,896]{2,1,0:T(8,128)(2,1)} %bitcast.289, ...), custom_call_target="tpu_custom_call" | custom-call | tf_op jit(solution)/shard_map/pallas_call | solution.py:88
  78.1 57.0 %shard_map.357 = (bf16[8,64,1024]{2,1,0:T(8,128)(2,1)}, bf16[4,8,32,896]{3,2,1,0:T(8,128)(2,1)}, bf16[4,8,32,1024]{3,2,1,0:T(8,128)(2,1)}) custom-call(bf16[8,64,1024]{2,1,0:T(8,128)(2,1)} %bitcast.302, bf16[8,32,896]{2,1,0:T(8,128)(2,1)} %get-tuple-element.51.refs_1_, bf16[8,32,1024]{2,1,0:T(8,128)(2,1)} %get-tuple-element.52.refs_2_), custom_call_target="tpu_custom_call" | custom-call | tf_op jit(solution)/shard_map/pallas_call | solution.py:88
  137.5 35.8 %shard_map.358 = bf16[8,64,1024]{2,1,0:T(8,128)(2,1)} custom-call(bf16[64,1024]{1,0:T(8,128)(2,1)} %multiply_convert_fusion.12.refs_0_), custom_call_target="tpu_custom_call" | custom-call | tf_op jit(solution)/shard_map/pallas_call | solution.py:88
  194.1 6.2 fusion.78
  206.0 50.0 %shard_map.359 = (bf16[8,64,1024]{2,1,0:T(8,128)(2,1)}, f32[8,8,128]{2,1,0:T(8,128)}) custom-call(bf16[8,64,1024]{2,1,0:T(8,128)(2,1)} %bitcast.279, f32[8,8,128]{2,1,0:T(8,128)} %pad.58.refs_1_), custom_call_target="tpu_custom_call" | custom-call | tf_op jit(solution)/shard_map/pallas_call | solution.py:88
  262.8 27.9 %shard_map.360 = (bf16[8,64,1024]{2,1,0:T(8,128)(2,1)}, f32[8,8,128]{2,1,0:T(8,128)}) custom-call(bf16[64,1024]{1,0:T(8,128)(2,1)} %add_convert_fusion.2.refs_0_, f32[8,128]{1,0:T(8,128)} %pad_bitcast_fusion.2.refs_1_), custom_call_target="tpu_custom_call" | custom-call | tf_op jit(solution)/shard_map/pallas_call | solution.py:88
  294.9 18.8 %shard_map.361 = bf16[8,64,1024]{2,1,0:T(8,128)(2,1)} custom-call(bf16[8,64,1024]{2,1,0:T(8,128)(2,1)} %bitcast.303), custom_call_target="tpu_custom_call" | custom-call | tf_op jit(solution)/shard_map/pallas_call | solution.py:88
  327.3 10.3 reshape.543
  337.6 6.1 fusion.89
  357.8 13.3 fusion.22
  374.8 9.6 convert_bitcast_fusion.5
  394.7 38.9 %all-gather.12.cloned.1.call-done = bf16[2048,1024]{1,0:T(8,128)(2,1)} async-done(((bf16[512,1024]{1,0:T(8,128)(2,1)}), bf16[2048,1024]{1,0:T(8,128)(2,1)}) %all-gather.12.cloned.1.call-update) | async-done | bytes 4194320 | tf_op jit(solution)/shard_map/all_gather | solution.py:298
  433.6 10.6 fusion.161
  444.2 40.7 %all-gather.16.cloned.1.call-done = bf16[1024,1024]{1,0:T(8,128)(2,1)} async-done(((bf16[128,1024]{1,0:T(8,128)(2,1)}), bf16[1024,1024]{1,0:T(8,128)(2,1)}) %all-gather.16.cloned.1.call-update) | async-done | bytes 2097168 | tf_op jit(solution)/shard_map/all_gather | solution.py:217
  484.9 10.6 fusion.162
  495.5 40.9 %all-gather.18.cloned.1.call-done = bf16[1024,1024]{1,0:T(8,128)(2,1)} async-done(((bf16[1024,128]{1,0:T(8,128)(2,1)}), bf16[1024,1024]{1,0:T(8,128)(2,1)}) %all-gather.18.cloned.1.call-update) | async-done | bytes 2097168 | tf_op jit(solution)/shard_map/all_gather | solution.py:218
  536.3 34.8 %all-gather.20.cloned.1.call-done = bf16[2048,1024]{1,0:T(8,128)(2,1)} async-done(((bf16[512,1024]{1,0:T(8,128)(2,1)}), bf16[2048,1024]{1,0:T(8,128)(2,1)}) %all-gather.20.cloned.1.call-update) | async-done | bytes 4194320 | tf_op jit(solution)/shard_map/all_gather | solution.py:221
  571.2 16.9 %multiply_convert_fusion = (bf16[2048,1024]{1,0:T(8,128)(2,1)}, bf16[2048,1024]{1,0:T(8,128)(2,1)}, bf16[2048,1024]{1,0:T(8,128)(2,1)}) fusion(f32[2048,1024]{1,0:T(8,128)} %fusion.161, f32[2048,1024]{1,0:T(8,128)} %fusion.162, bf16[2048,1024]{1,0:T(8,128)(2,1)} %all-gather.20.cloned.1.call-done, bf16[1024,1024]{1,0:T(8,128)(2,1)} %all-gather.18.cloned.1.call-done), kind=kOutput, calls=%fused_computation.3 | convolution fusion | flops 4326424576 | bytes 35651584 | tf_op jit(solution)/shard_map/dot_general | solution.py:107
  588.0 8.0 convolution_convert_fusion.2
  600.1 9.4 convolution_convert_fusion.4
  609.8 9.4 convolution_convert_fusion.3
  619.3 7.3 fusion.163
  626.5 6.7 add_convert_fusion
  633.3 9.4 convolution_convert_fusion.1
  653.7 14.2 reduce-scatter.16.cloned.1.call-done
  669.8 68.2 %reduce-scatter.12.cloned.1.call-done = bf16[128,1024]{1,0:T(8,128)(2,1)} async-done(((bf16[1024,1024]{1,0:T(8,128)(2,1)}), bf16[128,1024]{1,0:T(8,128)(2,1)}) %reduce-scatter.12.cloned.1.call-update) | async-done | bytes 262160 | tf_op jit(solution)/shard_map/reduce_scatter | solution.py:324
  739.8 68.2 %reduce-scatter.14.cloned.1.call-done = bf16[128,1024]{1,0:T(8,128)(2,1)} async-done(((bf16[1024,1024]{1,0:T(8,128)(2,1)}), bf16[128,1024]{1,0:T(8,128)(2,1)}) %reduce-scatter.14.cloned.1.call-update) | async-done | bytes 262160 | tf_op jit(solution)/shard_map/reduce_scatter | solution.py:325
  809.8 44.2 %reduce-scatter.10.cloned.1.call-done = bf16[512,1024]{1,0:T(8,128)(2,1)} async-done(((bf16[2048,1024]{1,0:T(8,128)(2,1)}), bf16[512,1024]{1,0:T(8,128)(2,1)}) %reduce-scatter.10.cloned.1.call-update) | async-done | bytes 1048592 | tf_op jit(solution)/shard_map/reduce_scatter | solution.py:317
  856.0 45.2 %reduce-scatter.8.cloned.1.call-done = bf16[512,1024]{1,0:T(8,128)(2,1)} async-done(((bf16[2048,1024]{1,0:T(8,128)(2,1)}), bf16[512,1024]{1,0:T(8,128)(2,1)}) %reduce-scatter.8.cloned.1.call-update) | async-done | bytes 1048592 | tf_op jit(solution)/shard_map/reduce_scatter | solution.py:304
  910.7 9.7 fusion.33
  920.4 17.4 %convert_reduce_fusion.2 = (f32[64,16,8]{2,1,0:T(8,128)}, pred[64,16,8,8]{2,3,1,0:T(8,128)(4,1)S(1)}, f32[64,16,8]{2,1,0:T(8,128)}, f32[64,16,8,8]{2,3,1,0:T(8,128)}) fusion(f32[64,16,8]{2,1,0:T(8,128)S(1)} %get-tuple-element.150, f32[64,16,8,8]{2,3,1,0:T(8,128)S(1)} %copy-done.1, pred[8,8]{0,1:T(8,128)(4,1)S(1)} %iota_compare_fusion.1, ...), kind=kOutput, calls=%fused_computation.21 | convolution fusion | flops 50905088 | bytes 4915264 | tf_op jit(solution)/shard_map/transpose(jvp(phij,pjhd->pihd))/dot_general | solution.py:159
  943.8 9.5 fusion.27
  953.3 10.7 fusion.30
  974.4 5.1 copy.229
  984.3 5.1 copy.232
  989.4 5.4 reshape.550
  994.9 9.2 convolution_convert_fusion
  1004.1 7.9 multiply_reduce_fusion.3
  1012.0 7.6 pad_maximum_fusion
  1019.5 7.9 copy.331
  1032.5 94.6 %shard_map.362 = (bf16[8,64,1024]{2,1,0:T(8,128)(2,1)}, bf16[4,8,32,4096]{3,2,1,0:T(8,128)(2,1)}) custom-call(bf16[8,64,1024]{2,1,0:T(8,128)(2,1)} %bitcast.274, bf16[4,8,32,4096]{3,2,1,0:T(8,128)(2,1)} %bitcast.271), custom_call_target="tpu_custom_call" | custom-call | tf_op jit(solution)/shard_map/pallas_call | solution.py:88
  1127.1 7.0 reduce_sum.428.refs_1_
  1139.2 56.8 %shard_map.363 = (bf16[8,64,1024]{2,1,0:T(8,128)(2,1)}, bf16[8,32,4096]{2,1,0:T(8,128)(2,1)}, bf16[4,8,32,1024]{3,2,1,0:T(8,128)(2,1)}) custom-call(bf16[8,64,1024]{2,1,0:T(8,128)(2,1)} %bitcast.290, bf16[8,32,4096]{2,1,0:T(8,128)(2,1)} %reduce_sum.428.refs_1_, bf16[4,8,32,1024]{3,2,1,0:T(8,128)(2,1)} %convert_bitcast_fusion.4.refs_2_), custom_call_target="tpu_custom_call" | custom-call | tf_op jit(solution)/shard_map/pallas_call | solution.py:88
  1203.4 51.3 %shard_map.364 = (bf16[8,64,1024]{2,1,0:T(8,128)(2,1)}, f32[8,8,128]{2,1,0:T(8,128)}, bf16[8,32,1024]{2,1,0:T(8,128)(2,1)}) custom-call(bf16[64,1024]{1,0:T(8,128)(2,1)} %get-tuple-element.99.refs_0_, f32[8,128]{1,0:T(8,128)} %pad_bitcast_fusion.1.refs_1_, bf16[8,32,1024]{2,1,0:T(8,128)(2,1)} %reduce_sum.434.refs_2_), custom_call_target="tpu_custom_call" | custom-call | tf_op jit(solution)/shard_map/pallas_call | solution.py:88
  1260.8 7.5 fusion.26
  1300.0 32.0 %shard_map.365 = (bf16[8,64,1024]{2,1,0:T(8,128)(2,1)}, bf16[4,64,1024]{2,1,0:T(8,128)(2,1)}, bf16[4,8,32,896]{3,2,1,0:T(8,128)(2,1)}) custom-call(bf16[8,64,1024]{2,1,0:T(8,128)(2,1)} %bitcast.300, bf16[4,64,1024]{2,1,0:T(8,128)(2,1)} %bitcast.284, bf16[4,8,32,896]{3,2,1,0:T(8,128)(2,1)} %convert_bitcast_fusion.6.refs_2_), custom_call_target="tpu_custom_call" | custom-call | tf_op jit(solution)/shard_map/pallas_call | solution.py:88
  1339.4 34.8 %shard_map.366 = (bf16[8,64,1024]{2,1,0:T(8,128)(2,1)}, f32[4,136,128]{2,1,0:T(8,128)}, bf16[8,32,896]{2,1,0:T(8,128)(2,1)}) custom-call(bf16[64,1024]{1,0:T(8,128)(2,1)} %fusion.105.refs_0_, f32[136,128]{1,0:T(8,128)} %pad_bitcast_fusion.refs_1_, bf16[8,32,896]{2,1,0:T(8,128)(2,1)} %reduce_sum.537.refs_2_), custom_call_target="tpu_custom_call" | custom-call | tf_op jit(solution)/shard_map/pallas_call | solution.py:88
  1383.8 37.8 %shard_map.367 = (bf16[8,64,1024]{2,1,0:T(8,128)(2,1)}, bf16[4,256,1024]{2,1,0:T(8,128)(2,1)}, f32[8,136,128]{2,1,0:T(8,128)}) custom-call(bf16[8,64,1024]{2,1,0:T(8,128)(2,1)} %bitcast.301, bf16[4,256,1024]{2,1,0:T(8,128)(2,1)} %bitcast.280, f32[136,128]{1,0:T(8,128)} %reduce_sum.538.refs_2_), custom_call_target="tpu_custom_call" | custom-call | tf_op jit(solution)/shard_map/pallas_call | solution.py:88
  (422 shorter events, 247.1 us)
Async XLA Ops:
  7.2 315.9 %all-gather.10.cloned.1.call-start = ((), (), s32[]{:S(2)}) async-start(), calls=%async_computation.6 | async-start | bytes 2162688 | tf_op jit(solution)/shard_map/all_gather | solution.py:214
  7.9 319.4 %all-gather.8.cloned.1.call-start = ((), (), s32[]{:S(2)}) async-start(), calls=%async_computation.5 | async-start | bytes 6488064 | tf_op jit(solution)/shard_map/all_gather | solution.py:213
  8.7 386.0 %all-gather.14.cloned.1.call-start = ((), (), s32[]{:S(2)}) async-start(), calls=%async_computation.8 | async-start | bytes 2359296 | tf_op jit(solution)/shard_map/all_gather | solution.py:216
  9.4 424.1 %all-gather.12.cloned.1.call-start = ((), (), s32[]{:S(2)}) async-start(), calls=%async_computation.7 | async-start | bytes 5242880 | tf_op jit(solution)/shard_map/all_gather | solution.py:298
  74.0 62.7 %copy-start.53 = (f32[1024]{0:T(1024)S(1)}, f32[1024]{0:T(1024)}, u32[]{:S(2)}) copy-start(f32[1024]{0:T(1024)} %param.32) | copy-start | bytes 12292
  136.6 125.5 %copy-start.8 = (f32[64,1024]{1,0:T(8,128)}, f32[64,1024]{1,0:T(8,128)S(1)}, u32[]{:S(2)}) copy-start(f32[64,1024]{1,0:T(8,128)S(1)} %convert_reduce_fusion.6) | copy-start | bytes 786436
  136.7 36.6 %copy-start.77 = (f32[64]{0:T(128)}, f32[64]{0:T(128)S(1)}, u32[]{:S(2)}) copy-start(f32[64]{0:T(128)S(1)} %multiply_reduce_fusion.17) | copy-start | bytes 772
  136.7 36.5 %copy-start.71 = (f32[64]{0:T(128)}, f32[64]{0:T(128)S(1)}, u32[]{:S(2)}) copy-start(f32[64]{0:T(128)S(1)} %fusion.132) | copy-start | bytes 772
  180.1 13.9 copy-start.6
  180.3 13.7 copy-start.55
  180.3 13.7 copy-start.57
  180.3 13.7 copy-start.59
  180.3 13.7 copy-start.61
  180.3 13.7 copy-start.89
  200.6 55.4 %copy-start.36 = (f32[512,256]{1,0:T(8,128)}, f32[512,256]{1,0:T(8,128)S(1)}, u32[]{:S(2)}) copy-start(f32[512,256]{1,0:T(8,128)S(1)} %copy.217) | copy-start | bytes 1572868
  202.1 60.0 %copy-start.19 = (f32[512,256]{1,0:T(8,128)}, f32[512,256]{1,0:T(8,128)S(1)}, u32[]{:S(2)}) copy-start(f32[512,256]{1,0:T(8,128)S(1)} %get-tuple-element.107) | copy-start | bytes 1572868
  202.8 59.2 %copy-start.65 = (f32[256]{0:T(256)}, f32[256]{0:T(256)S(1)}, u32[]{:S(2)}) copy-start(f32[256]{0:T(256)S(1)} %dynamic_slice.23) | copy-start | bytes 3076
  257.4 37.4 %copy-start.26 = (f32[64,1024]{1,0:T(8,128)}, f32[64,1024]{1,0:T(8,128)S(1)}, u32[]{:S(2)}) copy-start(f32[64,1024]{1,0:T(8,128)S(1)} %convert_reduce_fusion.5) | copy-start | bytes 786436
  294.9 23.7 %copy-start.63 = (f32[1024]{0:T(1024)S(1)}, f32[1024]{0:T(1024)}, u32[]{:S(2)}) copy-start(f32[1024]{0:T(1024)} %param.39) | copy-start | bytes 12292
  371.1 13.4 copy-start
  392.5 92.4 %all-gather.16.cloned.1.call-start = ((), (), s32[]{:S(2)}) async-start(), calls=%async_computation.9 | async-start | bytes 2359296 | tf_op jit(solution)/shard_map/all_gather | solution.py:217
  393.1 143.3 %all-gather.18.cloned.1.call-start = ((), (), s32[]{:S(2)}) async-start(), calls=%async_computation.10 | async-start | bytes 2359296 | tf_op jit(solution)/shard_map/all_gather | solution.py:218
  393.7 177.5 %all-gather.20.cloned.1.call-start = ((), (), s32[]{:S(2)}) async-start(), calls=%async_computation.12 | async-start | bytes 5242880 | tf_op jit(solution)/shard_map/all_gather | solution.py:221
  394.4 273.5 %reduce-scatter.16.cloned.1.call-start = ((), (), s32[]{:S(2)}) async-start(), calls=%async_computation.16 | async-start | bytes 2359296
  571.2 16.9 %copy-start.81 = (bf16[2048,1024]{1,0:T(8,128)(2,1)S(1)}, bf16[2048,1024]{1,0:T(8,128)(2,1)}, u32[]{:S(2)}) copy-start(bf16[2048,1024]{1,0:T(8,128)(2,1)} %all-gather.20.cloned.1.call-done) | copy-start | bytes 12582916
  600.1 138.0 %reduce-scatter.12.cloned.1.call-start = ((), (), s32[]{:S(2)}) async-start(), calls=%async_computation.14 | async-start | bytes 2359296 | tf_op jit(solution)/shard_map/reduce_scatter | solution.py:324
  609.5 198.5 %reduce-scatter.14.cloned.1.call-start = ((), (), s32[]{:S(2)}) async-start(), calls=%async_computation.15 | async-start | bytes 2359296 | tf_op jit(solution)/shard_map/reduce_scatter | solution.py:325
  619.2 234.9 %reduce-scatter.10.cloned.1.call-start = ((), (), s32[]{:S(2)}) async-start(), calls=%async_computation.13 | async-start | bytes 5242880 | tf_op jit(solution)/shard_map/reduce_scatter | solution.py:317
  633.2 267.9 %reduce-scatter.8.cloned.1.call-start = ((), (), s32[]{:S(2)}) async-start(), calls=%async_computation.11 | async-start | bytes 5242880 | tf_op jit(solution)/shard_map/reduce_scatter | solution.py:304
  953.3 10.7 copy-start.13
  953.3 10.7 copy-start.39
  1139.2 116.4 %copy-start.16 = (f32[512,512]{1,0:T(8,128)S(1)}, f32[512,512]{1,0:T(8,128)}, u32[]{:S(2)}) copy-start(f32[512,512]{1,0:T(8,128)} %copy-done.15) | copy-start | bytes 3145732
  1139.2 116.4 %copy-start.18 = (f32[512,896]{1,0:T(8,128)S(1)}, f32[512,896]{1,0:T(8,128)}, u32[]{:S(2)}) copy-start(f32[512,896]{1,0:T(8,128)} %copy-done.17) | copy-start | bytes 5505028
  1139.2 116.4 %copy-start.20 = (f32[512,256]{1,0:T(8,128)S(1)}, f32[512,256]{1,0:T(8,128)}, u32[]{:S(2)}) copy-start(f32[512,256]{1,0:T(8,128)} %copy-done.19) | copy-start | bytes 1572868
  1139.2 116.4 %copy-start.66 = (f32[256]{0:T(256)S(1)}, f32[256]{0:T(256)}, u32[]{:S(2)}) copy-start(f32[256]{0:T(256)} %copy-done.65) | copy-start | bytes 3076
  1202.8 58.0 %copy-start.68 = (f32[4,512]{1,0:T(4,128)S(1)}, f32[4,512]{1,0:T(4,128)}, u32[]{:S(2)}) copy-start(f32[4,512]{1,0:T(4,128)} %copy-done.67) | copy-start | bytes 24580
  1202.8 58.0 %copy-start.70 = (f32[1,4,4,128]{3,1,2,0:T(4,128)S(1)}, f32[1,4,4,128]{3,1,2,0:T(4,128)}, u32[]{:S(2)}) copy-start(f32[1,4,4,128]{3,1,2,0:T(4,128)} %copy-done.69) | copy-start | bytes 24580
  1260.8 12.0 copy-start.44
  1297.4 36.0 %copy-start.9 = (f32[64,1024]{1,0:T(8,128)S(1)}, f32[64,1024]{1,0:T(8,128)}, u32[]{:S(2)}) copy-start(f32[64,1024]{1,0:T(8,128)} %copy-done.8) | copy-start | bytes 786436
  1297.4 36.0 %copy-start.54 = (f32[1024]{0:T(1024)S(1)}, f32[1024]{0:T(1024)}, u32[]{:S(2)}) copy-start(f32[1024]{0:T(1024)} %param.32) | copy-start | bytes 12292
  1297.4 36.0 %copy-start.72 = (f32[64]{0:T(128)S(1)}, f32[64]{0:T(128)}, u32[]{:S(2)}) copy-start(f32[64]{0:T(128)} %copy-done.71) | copy-start | bytes 772
  1300.0 34.2 %copy-start.80 = (f32[32]{0:T(128)S(1)}, f32[32]{0:T(128)}, u32[]{:S(2)}) copy-start(f32[32]{0:T(128)} %param.36) | copy-start | bytes 388
  1300.0 38.6 %copy-start.78 = (f32[64]{0:T(128)S(1)}, f32[64]{0:T(128)}, u32[]{:S(2)}) copy-start(f32[64]{0:T(128)} %copy-done.77) | copy-start | bytes 772
  1300.0 38.6 %copy-start.28 = (f32[64,1024]{1,0:T(8,128)S(1)}, f32[64,1024]{1,0:T(8,128)}, u32[]{:S(2)}) copy-start(f32[64,1024]{1,0:T(8,128)} %copy-done.27) | copy-start | bytes 786436
  1333.5 43.4 %copy-start.84 = (bf16[8,64,1024]{2,1,0:T(8,128)(2,1)S(1)}, bf16[8,64,1024]{2,1,0:T(8,128)(2,1)}, u32[]{:S(2)}) copy-start(bf16[8,64,1024]{2,1,0:T(8,128)(2,1)} %get-tuple-element.49) | copy-start | bytes 3145732
  1383.2 43.4 %copy-start.33 = (bf16[8,32,4096]{2,1,0:T(8,128)(2,1)S(1)}, bf16[8,32,4096]{2,1,0:T(8,128)(2,1)}, u32[]{:S(2)}) copy-start(bf16[8,32,4096]{2,1,0:T(8,128)(2,1)} %get-tuple-element.76) | copy-start | bytes 6291460
  1383.8 45.6 %slice-start = ((f32[32,8,896]{2,0,1:T(8,128)}), f32[32,8,4]{2,0,1:T(8,128)S(1)}, s32[]{:S(2)}) async-start(f32[32,8,896]{2,0,1:T(8,128)} %copy-done.25), calls=%async_computation.17 | async-start | bytes 262144 | tf_op jit(solution)/shard_map/slice | solution.py:455
  1421.6 10.2 copy-start.40
  (63 other events, 316.7 us)
Sparse Core Ops, SparseCore 0:
  10.9 76.3 all-gather.9
  90.1 92.4 all-gather.7
  184.8 63.8 all-gather.13
  392.6 40.8 all-gather.11
  435.5 49.2 all-gather.15
  486.8 49.5 all-gather.17
  538.5 32.6 all-gather.19
  600.2 67.6 reduce-scatter.15
  671.4 66.5 reduce-scatter.11
  741.4 66.5 reduce-scatter.13
  810.6 43.4 reduce-scatter.9
  856.6 44.5 reduce-scatter.7

commit v2 on v1

--- a/solution.py
+++ b/solution.py
@@ -18,11 +18,30 @@
 HEAD_A = 64
 PROJ = 4384
 LANE = 128
+VMEM_LIMIT = 60 * 2**20
 
 HIGH = lax.Precision.HIGHEST
 EPSILON = 1e-05
 BF = jnp.bfloat16
 F32 = jnp.float32
+
+
+MESH = pl.DeviceIdType.MESH
+
+
+def greet(axes, me, sizes):
+    barrier = pltpu.get_barrier_semaphore()
+    arrivals = 0
+    for axis in axes:
+        for k in range(1, sizes[axis]):
+            pl.semaphore_signal(
+                barrier,
+                inc=1,
+                device_id={axis: lax.rem(me[axis] + k, sizes[axis])},
+                device_id_type=MESH,
+            )
+        arrivals += sizes[axis] - 1
+    pl.semaphore_wait(barrier, arrivals)
 
 
 def exchange_kernel(plan, sizes, *refs):
@@ -32,56 +51,81 @@
     local_sem = sems[0]
     axes = sorted({axis for _, axis in plan})
     me = {axis: lax.axis_index(axis) for axis in axes}
-    barrier = pltpu.get_barrier_semaphore()
-    total = 0
-    for axis in axes:
-        for k in range(1, sizes[axis]):
-            pl.semaphore_signal(
-                barrier,
-                inc=1,
-                device_id={axis: lax.rem(me[axis] + k, sizes[axis])},
-                device_id_type=pl.DeviceIdType.MESH,
-            )
-        total += sizes[axis] - 1
-    pl.semaphore_wait(barrier, total)
+    greet(axes, me, sizes)
+
+    def slot(index, peer):
+        kind = plan[index][0]
+        if kind == "a2a":
+            return sources[index].at[peer]
+        if kind == "a2a1":
+            return sources[index].at[:, peer]
+        return sources[index]
+
     copies = []
+    relays = []
     for index, (kind, axis) in enumerate(plan):
         send, recv = sems[1 + 2 * index], sems[2 + 2 * index]
-        for k in range(1, sizes[axis]):
-            peer = lax.rem(me[axis] + k, sizes[axis])
-            source = sources[index].at[peer] if kind == "a2a" else sources[index]
+        here = me[axis]
+
+        def remote(source, target, number, peer):
             copy = pltpu.make_async_remote_copy(
                 src_ref=source,
-                dst_ref=targets[index].at[me[axis]],
-                send_sem=send.at[k - 1],
-                recv_sem=recv.at[k - 1],
+                dst_ref=target,
+                send_sem=send.at[number],
+                recv_sem=recv.at[number],
                 device_id={axis: peer},
-                device_id_type=pl.DeviceIdType.MESH,
+                device_id_type=MESH,
             )
             copy.start()
-            copies.append(copy)
+            return copy
+
+        if kind == "agh":
+            core = lax.rem(here, 2)
+            chips = sizes[axis] // 2
+            twin = here + 1 - 2 * core
+            for k in range(1, chips):
+                peer = lax.rem(here + 2 * k, sizes[axis])
+                came = lax.rem(here + sizes[axis] - 2 * k, sizes[axis])
+                copy = remote(sources[index], targets[index].at[here], k, peer)
+                relays.append((copy, targets[index].at[came], chips - 1 + k, twin, remote))
+            copies.append(remote(sources[index], targets[index].at[here], 0, twin))
+        else:
+            for k in range(1, sizes[axis]):
+                peer = lax.rem(here + k, sizes[axis])
+                copies.append(remote(slot(index, peer), targets[index].at[here], k - 1, peer))
     own = []
     for index, (kind, axis) in enumerate(plan):
-        source = sources[index].at[me[axis]] if kind == "a2a" else sources[index]
-        copy = pltpu.make_async_copy(source, targets[index].at[me[axis]], local_sem.at[index])
+        here = me[axis]
+        copy = pltpu.make_async_copy(
+            slot(index, here), targets[index].at[here], local_sem.at[index]
+        )
         copy.start()
         own.append(copy)
+    for copy, block, number, twin, remote in relays:
+        copy.wait_recv()
+        copies.append(remote(block, block, number, twin))
     for copy in own:
         copy.wait()
     for copy in copies:
         copy.wait()
+    for copy, *_ in relays:
+        copy.wait_send()
 
 
 def exchange(ident, *steps):
     plan = tuple((kind, axis) for kind, axis, _ in steps)
     arrays = [array for _, _, array in steps]
     sizes = {axis: lax.axis_size(axis) for _, axis in plan}
-    shapes = [
-        jax.ShapeDtypeStruct(
-            array.shape if kind == "a2a" else (sizes[axis],) + array.shape, array.dtype
-        )
-        for kind, axis, array in steps
-    ]
+    shapes = []
+    moved = 0
+    for kind, axis, array in steps:
+        shape = array.shape
+        if kind in ("ag", "agh"):
+            shape = (sizes[axis],) + shape
+        elif kind == "a2a1":
+            shape = (shape[1], shape[0]) + shape[2:]
+        shapes.append(jax.ShapeDtypeStruct(shape, array.dtype))
+        moved += shapes[-1].size * array.dtype.itemsize
     scratch = [pltpu.SemaphoreType.DMA((len(plan),))]
     for _, axis in plan:
         scratch += [pltpu.SemaphoreType.DMA((sizes[axis] - 1,))] * 2
@@ -92,7 +136,477 @@
         out_specs=[pl.BlockSpec(memory_space=pl.ANY)] * len(plan),
         scratch_shapes=scratch,
         compiler_params=pltpu.CompilerParams(collective_id=ident, has_side_effects=True),
+        cost_estimate=pl.CostEstimate(flops=0, bytes_accessed=64 * moved, transcendentals=0),
     )(*arrays)
+
+
+def attend_forward_kernel(
+    local_ref, gain_ref, feed_gain_ref, w_ref, low_ref, qkv_ref, attended_ref, after_ref, feed_ref
+):
+    rows = local_ref.shape[0]
+    step = min(rows, 256)
+    mask = patch_mask(LANE)
+    first = lax.broadcasted_iota(jnp.int32, (LANE, LANE), 1) < HEAD_A
+
+    def some(index, _):
+        at = pl.ds(pl.multiple_of(index * step, step), step)
+        local = local_ref[at, :]
+        low = root_norm(local, gain_ref[...]).astype(BF)
+        low_ref[at, :] = low
+        qkv_ref[at, :] = product(low, w_ref[:, : 3 * D]).astype(BF)
+
+        def heads(inner, _):
+            within = pl.ds(pl.multiple_of(index * step + inner * LANE, LANE), LANE)
+            for pair in range(D // LANE):
+                lanes = slice(pair * LANE, (pair + 1) * LANE)
+                query = qkv_ref[within, lanes]
+                keyed = qkv_ref[within, D + pair * LANE : D + (pair + 1) * LANE]
+                valued = qkv_ref[within, 2 * D + pair * LANE : 2 * D + (pair + 1) * LANE]
+                results = []
+                for half in (first, ~first):
+                    probs = patch_probs(jnp.where(half, query, 0), keyed, mask)
+                    results.append(product(probs.astype(BF), valued))
+                attended_ref[within, lanes] = jnp.where(first, results[0], results[1]).astype(BF)
+            return 0
+
+        lax.fori_loop(0, step // LANE, heads, 0)
+        after = local + product(attended_ref[at, :], w_ref[:, 3 * D :])
+        after_ref[at, :] = after
+        feed_ref[at, :] = root_norm(after, feed_gain_ref[...]).astype(BF)
+        return 0
+
+    lax.fori_loop(0, rows // step, some, 0)
+
+
+def patch_mask(count):
+    row = lax.broadcasted_iota(jnp.int32, (count, count), 0)
+    column = lax.broadcasted_iota(jnp.int32, (count, count), 1)
+    return (row // PATCH == column // PATCH) & (column <= row)
+
+
+def patch_probs(query, keyed, mask):
+    scores = jnp.where(mask, right_product(query, keyed) * HEAD_A ** (-0.5), -1e30)
+    expo = jnp.exp(scores - jnp.max(scores, axis=-1, keepdims=True))
+    return expo / jnp.sum(expo, axis=-1, keepdims=True)
+
+
+def attend_forward(local_in, norm_attend, norm_feed, w_attend):
+    rows = local_in.shape[0]
+    return pl.pallas_call(
+        attend_forward_kernel,
+        out_shape=[
+            jax.ShapeDtypeStruct((rows, D), BF),
+            jax.ShapeDtypeStruct((rows, 3 * D), BF),
+            jax.ShapeDtypeStruct((rows, D), BF),
+            jax.ShapeDtypeStruct((rows, D), F32),
+            jax.ShapeDtypeStruct((rows, D), BF),
+        ],
+        in_specs=[pl.BlockSpec(memory_space=pltpu.VMEM)] * 4,
+        out_specs=[pl.BlockSpec(memory_space=pltpu.VMEM)] * 5,
+        compiler_params=pltpu.CompilerParams(vmem_limit_bytes=VMEM_LIMIT),
+        cost_estimate=pl.CostEstimate(
+            flops=2 * rows * D * 4 * D, bytes_accessed=24 * D * D, transcendentals=rows * 16 * LANE
+        ),
+    )(local_in, norm_attend[None], norm_feed[None], w_attend)
+
+
+def norm_back(values, gain, grad):
+    scale = lax.rsqrt(jnp.mean(values * values, axis=-1, keepdims=True) + EPSILON)
+    scaled = grad * gain
+    along = jnp.mean(scaled * values, axis=-1, keepdims=True)
+    return scale * scaled - values * (scale * scale * scale * along), grad * values * scale
+
+
+def attend_backward_kernel(
+    grad_feed_ref,
+    grad_final_ref,
+    local_ref,
+    after_ref,
+    low_ref,
+    qkv_ref,
+    attended_ref,
+    gain_ref,
+    feed_gain_ref,
+    w_ref,
+    grad_local_ref,
+    grad_slots_ref,
+    grad_w_ref,
+    grad_gain_ref,
+    grad_feed_gain_ref,
+    grads_ref,
+):
+    rows = local_ref.shape[0]
+    step = min(rows, 256)
+    mask = patch_mask(LANE)
+    first = lax.broadcasted_iota(jnp.int32, (LANE, LANE), 1) < HEAD_A
+    grad_gain_ref[...] = jnp.zeros_like(grad_gain_ref)
+    grad_feed_gain_ref[...] = jnp.zeros_like(grad_feed_gain_ref)
+
+    def some(index, _):
+        at = pl.ds(pl.multiple_of(index * step, step), step)
+        grad_after, gains = norm_back(after_ref[at, :], feed_gain_ref[...], grad_feed_ref[at, :])
+        grad_feed_gain_ref[...] += jnp.sum(gains, axis=0, keepdims=True)
+        grad_after = grad_after + grad_final_ref[at, :].astype(F32)
+        grad_low = grad_after.astype(BF)
+        grads_ref[at, 3 * D :] = grad_low
+        grad_attended = right_product(grad_low, w_ref[:, 3 * D :]).astype(BF)
+        grads_ref[at, :D] = grad_attended
+
+        def heads(inner, _):
+            within = pl.ds(pl.multiple_of(index * step + inner * LANE, LANE), LANE)
+            for pair in range(D // LANE):
+                lanes = slice(pair * LANE, (pair + 1) * LANE)
+                query = qkv_ref[within, lanes]
+                keyed = qkv_ref[within, D + pair * LANE : D + (pair + 1) * LANE]
+                valued = qkv_ref[within, 2 * D + pair * LANE : 2 * D + (pair + 1) * LANE]
+                grad = grads_ref[within, lanes]
+                parts = []
+                for half in (first, ~first):
+                    probs = patch_probs(jnp.where(half, query, 0), keyed, mask)
+                    grad_probs = right_product(jnp.where(half, grad, 0), valued)
+                    inside = jnp.sum(grad_probs * probs, axis=-1, keepdims=True)
+                    grad_scores = (probs * (grad_probs - inside) * HEAD_A ** (-0.5)).astype(BF)
+                    parts.append(
+                        (
+                            product(grad_scores, keyed),
+                            left_product(grad_scores, query),
+                            left_product(probs.astype(BF), grad),
+                        )
+                    )
+                for number in range(3):
+                    there = slice(number * D + pair * LANE, number * D + (pair + 1) * LANE)
+                    grads_ref[within, there] = jnp.where(
+                        first, parts[0][number], parts[1][number]
+                    ).astype(BF)
+            return 0
+
+        lax.fori_loop(0, step // LANE, heads, 0)
+        grad_normed = right_product(grads_ref[at, : 3 * D], w_ref[:, : 3 * D])
+        grad_local, gains = norm_back(local_ref[at, :], gain_ref[...], grad_normed)
+        grad_gain_ref[...] += jnp.sum(gains, axis=0, keepdims=True)
+        grad_local = grad_after + grad_local
+        grad_local_ref[at, :] = grad_local
+        grad_slots_ref[at, :] = grad_local.astype(BF)
+        return 0
+
+    lax.fori_loop(0, rows // step, some, 0)
+
+    def columns(index, _):
+        at = pl.ds(pl.multiple_of(index * 256, 256), 256)
+        grad_w_ref[at, : 3 * D] = left_product(low_ref[:, at], grads_ref[:, : 3 * D]).astype(BF)
+        grad_w_ref[at, 3 * D :] = left_product(attended_ref[:, at], grads_ref[:, 3 * D :]).astype(BF)
+        return 0
+
+    lax.fori_loop(0, D // 256, columns, 0)
+
+
+def attend_backward(grad_feed, grad_final, local_in, after, low, qkv, attended, gain, feed_gain, w):
+    rows = local_in.shape[0]
+    return pl.pallas_call(
+        attend_backward_kernel,
+        out_shape=[
+            jax.ShapeDtypeStruct((rows, D), F32),
+            jax.ShapeDtypeStruct((rows, D), BF),
+            jax.ShapeDtypeStruct((D, 4 * D), BF),
+            jax.ShapeDtypeStruct((1, D), F32),
+            jax.ShapeDtypeStruct((1, D), F32),
+        ],
+        in_specs=[pl.BlockSpec(memory_space=pltpu.VMEM)] * 10,
+        out_specs=[pl.BlockSpec(memory_space=pltpu.VMEM)] * 5,
+        scratch_shapes=[pltpu.VMEM((rows, 4 * D), BF)],
+        compiler_params=pltpu.CompilerParams(vmem_limit_bytes=VMEM_LIMIT),
+        cost_estimate=pl.CostEstimate(
+            flops=4 * rows * D * 4 * D, bytes_accessed=40 * D * D, transcendentals=rows * 16 * LANE
+        ),
+    )(grad_feed, grad_final, local_in, after, low, qkv, attended, gain[None], feed_gain[None], w)
+
+
+def feed_kernel(
+    n_mp,
+    x_ref,
+    c_ref,
+    w_ref,
+    out_ref,
+    grad_feed_ref,
+    grads_ref,
+    held,
+    hidden,
+    grad_gate,
+    grad_up,
+    grad_held,
+    paired,
+    arrived,
+    staged,
+    own_sem,
+    stage_sems,
+    ag_send,
+    ag_recv,
+    pair_send,
+    pair_recv,
+    far_send,
+    far_recv,
+):
+    rows = x_ref.shape[0]
+    chips = n_mp // 2
+    units = w_ref.shape[-1]
+    here = lax.axis_index("mp")
+    core = lax.rem(here, 2)
+    twin = here + 1 - 2 * core
+    step = min(rows, 256)
+    greet(("mp",), {"mp": here}, {"mp": n_mp})
+
+    def block(owner):
+        return pl.ds(pl.multiple_of(owner * rows, rows), rows)
+
+    def remote(source, target, send, recv, peer):
+        copy = pltpu.make_async_remote_copy(
+            src_ref=source,
+            dst_ref=target,
+            send_sem=send,
+            recv_sem=recv,
+            device_id={"mp": peer},
+            device_id_type=MESH,
+        )
+        copy.start()
+        return copy
+
+    own = pltpu.make_async_copy(x_ref, held.at[block(here)], own_sem)
+    own.start()
+    far = [lax.rem(here + 2 * k, n_mp) for k in range(chips)]
+    came = [lax.rem(here + n_mp - 2 * k, n_mp) for k in range(chips)]
+    direct = [
+        remote(x_ref, held.at[block(here)], ag_send.at[k], ag_recv.at[k], far[k])
+        for k in range(1, chips)
+    ]
+    near = remote(x_ref, held.at[block(here)], ag_send.at[0], ag_recv.at[0], twin)
+
+    def weight(number):
+        return w_ref[:, number].reshape(D, units)
+
+    stored = []
+
+    def rows_of(owner):
+        number = len(stored)
+        slot = number % 2
+        if number >= 2:
+            stored[number - 2].wait()
+
+        def some(index, _):
+            local = pl.ds(pl.multiple_of(index * step, step), step)
+            at = pl.ds(pl.multiple_of(owner * rows + index * step, step), step)
+            x = held[at, :]
+            gate = product(x, weight(0))
+            up = product(x, weight(1))
+            sigmoid = jax.nn.sigmoid(gate)
+            silu = gate * sigmoid
+            low = (silu * up).astype(BF)
+            hidden[at, :] = low
+            grad_hidden = product(c_ref[at, :], weight(2))
+            gate_low = (grad_hidden * up * sigmoid * (1.0 + gate * (1.0 - sigmoid))).astype(BF)
+            up_low = (grad_hidden * silu).astype(BF)
+            grad_gate[at, :] = gate_low
+            grad_up[at, :] = up_low
+            staged[slot, local, :] = right_product(low, weight(2)).astype(BF)
+            grad_held[at, :] = (
+                right_product(gate_low, weight(0)) + right_product(up_low, weight(1))
+            ).astype(BF)
+            return 0
+
+        lax.fori_loop(0, rows // step, some, 0)
+        copy = pltpu.make_async_copy(
+            staged.at[slot], out_ref.at[block(owner)], stage_sems.at[number]
+        )
+        copy.start()
+        stored.append(copy)
+
+    def to_twin(owner, number):
+        return remote(
+            grad_held.at[block(owner)],
+            paired.at[number],
+            pair_send.at[number],
+            pair_recv.at[number],
+            twin,
+        )
+
+    own.wait()
+    rows_of(here)
+    near.wait_recv()
+    rows_of(twin)
+    pairs = [to_twin(twin, 0)]
+    relays = []
+    for k in range(1, chips):
+        direct[k - 1].wait_recv()
+        relays.append(
+            remote(
+                held.at[block(came[k])],
+                held.at[block(came[k])],
+                ag_send.at[chips - 1 + k],
+                ag_recv.at[chips - 1 + k],
+                twin,
+            )
+        )
+        rows_of(came[k])
+        relays[-1].wait_recv()
+        other = came[k] + 1 - 2 * core
+        rows_of(other)
+        pairs.append(to_twin(other, k))
+
+    def tiles(start, stop):
+        def some(index, _):
+            at = pl.ds(pl.multiple_of(index * LANE, LANE), LANE)
+            x = held[:, at]
+            grads_ref[0, at, :] = left_product(x, grad_gate[...]).astype(BF)
+            grads_ref[1, at, :] = left_product(x, grad_up[...]).astype(BF)
+            grads_ref[2, at, :] = left_product(c_ref[:, at], hidden[...]).astype(BF)
+            return 0
+
+        lax.fori_loop(start, stop, some, 0)
+
+    count = D // LANE
+    tiles(0, count // 4)
+    sends = []
+    for k in range(chips):
+        pairs[k].wait_recv()
+        at = block(came[k])
+        grad_held[at, :] = (grad_held[at, :].astype(F32) + paired[k].astype(F32)).astype(BF)
+        if k:
+            sends.append(
+                remote(
+                    grad_held.at[at],
+                    arrived.at[k - 1],
+                    far_send.at[k - 1],
+                    far_recv.at[k - 1],
+                    came[k],
+                )
+            )
+    tiles(count // 4, count)
+    total_here = grad_held[block(here), :].astype(F32)
+    for k in range(1, chips):
+        sends[k - 1].wait_recv()
+        total_here = total_here + arrived[k - 1].astype(F32)
+    grad_feed_ref[...] = total_here
+    near.wait_send()
+    for copy in direct + relays + pairs + sends:
+        copy.wait_send()
+    for copy in stored[-2:]:
+        copy.wait()
+
+
+def feed_section(ident, feed_low, grad_rows, weights):
+    n_mp = lax.axis_size("mp")
+    rows = feed_low.shape[0]
+    every = rows * n_mp
+    chips = n_mp // 2
+    units = weights.shape[-1]
+    dma = pltpu.SemaphoreType.DMA
+    vmem = pl.BlockSpec(memory_space=pltpu.VMEM)
+    return pl.pallas_call(
+        functools.partial(feed_kernel, n_mp),
+        out_shape=[
+            jax.ShapeDtypeStruct((every, D), BF),
+            jax.ShapeDtypeStruct((rows, D), F32),
+            jax.ShapeDtypeStruct((3, D, units), BF),
+        ],
+        in_specs=[vmem] * 3,
+        out_specs=[pl.BlockSpec(memory_space=pl.ANY), vmem, vmem],
+        scratch_shapes=[
+            pltpu.VMEM((every, D), BF),
+            pltpu.VMEM((every, units), BF),
+            pltpu.VMEM((every, units), BF),
+            pltpu.VMEM((every, units), BF),
+            pltpu.VMEM((every, D), BF),
+            pltpu.VMEM((chips, rows, D), BF),
+            pltpu.VMEM((chips - 1, rows, D), BF),
+            pltpu.VMEM((2, rows, D), BF),
+            dma,
+            dma((n_mp,)),
+            dma((n_mp - 1,)),
+            dma((n_mp - 1,)),
+            dma((chips,)),
+            dma((chips,)),
+            dma((chips - 1,)),
+            dma((chips - 1,)),
+        ],
+        compiler_params=pltpu.CompilerParams(
+            collective_id=ident, has_side_effects=True, vmem_limit_bytes=VMEM_LIMIT
+        ),
+        cost_estimate=pl.CostEstimate(
+            flops=18 * every * D * units, bytes_accessed=30 * D * D, transcendentals=every * units
+        ),
+    )(feed_low, grad_rows, weights)
+
+
+def pair_sum_kernel(n_mp, x_ref, out_ref, mine, paired, local_sems, pair_send, pair_recv, far_send, far_recv, own_sem):
+    chips = n_mp // 2
+    here = lax.axis_index("mp")
+    core = lax.rem(here, 2)
+    twin = here + 1 - 2 * core
+    greet(("mp",), {"mp": here}, {"mp": n_mp})
+    owners = [lax.rem(here + 2 * k, n_mp) for k in range(chips)]
+    pairs, loads = [], []
+    for k in range(chips):
+        copy = pltpu.make_async_remote_copy(
+            src_ref=x_ref.at[owners[k] + 1 - 2 * core],
+            dst_ref=paired.at[k],
+            send_sem=pair_send.at[k],
+            recv_sem=pair_recv.at[k],
+            device_id={"mp": twin},
+            device_id_type=MESH,
+        )
+        copy.start()
+        pairs.append(copy)
+        copy = pltpu.make_async_copy(x_ref.at[owners[k]], mine.at[k], local_sems.at[k])
+        copy.start()
+        loads.append(copy)
+    sends = []
+    for k in list(range(1, chips)) + [0]:
+        loads[k].wait()
+        pairs[k].wait_recv()
+        mine[k] = (mine[k].astype(F32) + paired[k].astype(F32)).astype(BF)
+        if k:
+            copy = pltpu.make_async_remote_copy(
+                src_ref=mine.at[k],
+                dst_ref=out_ref.at[k],
+                send_sem=far_send.at[k - 1],
+                recv_sem=far_recv.at[k - 1],
+                device_id={"mp": owners[k]},
+                device_id_type=MESH,
+            )
+        else:
+            copy = pltpu.make_async_copy(mine.at[0], out_ref.at[0], own_sem)
+        copy.start()
+        sends.append(copy)
+    for copy in sends:
+        copy.wait()
+    for copy in pairs:
+        copy.wait_send()
+
+
+def pair_sum(ident, x):
+    n_mp = lax.axis_size("mp")
+    chips = n_mp // 2
+    dma = pltpu.SemaphoreType.DMA
+    hbm = pl.BlockSpec(memory_space=pl.ANY)
+    return pl.pallas_call(
+        functools.partial(pair_sum_kernel, n_mp),
+        out_shape=jax.ShapeDtypeStruct((chips,) + x.shape[1:], BF),
+        in_specs=[hbm],
+        out_specs=hbm,
+        scratch_shapes=[
+            pltpu.VMEM((chips,) + x.shape[1:], BF),
+            pltpu.VMEM((chips,) + x.shape[1:], BF),
+            dma((chips,)),
+            dma((chips,)),
+            dma((chips,)),
+            dma((chips - 1,)),
+            dma((chips - 1,)),
+            dma,
+        ],
+        compiler_params=pltpu.CompilerParams(
+            collective_id=ident, has_side_effects=True, vmem_limit_bytes=VMEM_LIMIT
+        ),
+        cost_estimate=pl.CostEstimate(flops=0, bytes_accessed=64 * x.size, transcendentals=0),
+    )(x)
 
 
 def product(left, right):
@@ -142,22 +656,6 @@
     values = jnp.einsum("hts,shp->thp", weights, heads_x, precision=HIGH)
     values = values + skip_gain[None, :, None] * heads_x
     return values.reshape(count, inner) * jax.nn.silu(gate_part)
-
-
-def patch_attention(attend_proj):
-    count = attend_proj.shape[0]
-    patches = count // PATCH
-    query = attend_proj[:, :D].reshape(patches, PATCH, HEADS_A, HEAD_A)
-    keyed = attend_proj[:, D : 2 * D].reshape(patches, PATCH, HEADS_A, HEAD_A)
-    valued = attend_proj[:, 2 * D :].reshape(patches, PATCH, HEADS_A, HEAD_A)
-    scores = jnp.einsum("pihd,pjhd->phij", query, keyed, precision=HIGH) * HEAD_A ** (-0.5)
-    causal = jnp.arange(PATCH)[:, None] >= jnp.arange(PATCH)[None, :]
-    scores = jnp.where(causal, scores, -jnp.inf)
-    top = jnp.max(scores, axis=-1, keepdims=True)
-    expo = jnp.exp(scores - top)
-    probs = expo / jnp.sum(expo, axis=-1, keepdims=True)
-    result = jnp.einsum("phij,pjhd->pihd", probs, valued, precision=HIGH)
-    return result.reshape(count, D)
 
 
 def own_columns(array, place, width):
@@ -210,15 +708,14 @@
     step_pad = -heads % LANE
     cols = 2 * inner + 2 * STATE + heads + step_pad
 
-    w_attend = lax.all_gather(attend_in, ("dp", "mp"), axis=0, tiled=True).reshape(D, 3 * D)
-    w_attend_out = lax.all_gather(attend_out, ("dp", "mp"), axis=0, tiled=True).reshape(D, D)
-    w_gate, w_up, w_down = (
-        lax.all_gather(gate_weight, "dp", axis=0, tiled=True),
-        lax.all_gather(up_weight, "dp", axis=0, tiled=True),
-        lax.all_gather(down_weight, "dp", axis=1, tiled=True),
-    )
-    grad_final = cotangent[0].astype(F32) * keep
-    grad_feed_rows = lax.all_gather(grad_final.astype(BF), "mp", axis=0, tiled=True)
+    w_attend = lax.all_gather(
+        jnp.concatenate([attend_in.reshape(k_rows, -1), attend_out.reshape(k_rows, -1)], axis=1),
+        ("dp", "mp"),
+        axis=0,
+        tiled=True,
+    )
+    w_feed = lax.all_gather(jnp.stack([gate_weight, up_weight, down_weight.T]), "dp", axis=0)
+    grad_final = (cotangent[0].astype(F32) * keep).astype(BF)
 
     mixer_rows = mixer_in.reshape(k_rows, PROJ)
     shared = mixer_rows[:, 2 * INNER : 2 * INNER + 2 * STATE]
@@ -275,8 +772,11 @@
     own_gain = own_columns(norm_gated, place, inner)
     squares = jnp.sum(gated * gated, axis=1).reshape(n_dp, patches)
     parts = product((gated * own_gain).astype(BF), w_mixer_out).astype(BF)
-    parts, squares = exchange(
-        3, ("a2a", "dp", parts.reshape(n_dp, patches, D)), ("a2a", "dp", tucked(squares))
+    parts, squares, grad_feed_rows = exchange(
+        3,
+        ("a2a", "dp", parts.reshape(n_dp, patches, D)),
+        ("a2a", "dp", tucked(squares)),
+        ("agh", "mp", grad_final),
     )
     scale = lax.rsqrt(total(squares)[0, :patches] / INNER + EPSILON)
     unscaled = total(parts)
@@ -290,75 +790,47 @@
     (slots,) = exchange(5, ("a2a", "dp", slots.reshape(n_dp, patches, byte_cols)))
     local_in = inputs + slots.astype(F32).transpose(1, 0, 2).reshape(rows, D)
 
-    attend_low = root_norm(local_in, norm_attend).astype(BF)
-    attend_proj = product(attend_low, w_attend)
-    attended_low = patch_attention(attend_proj).astype(BF)
-    after_attend = local_in + product(attended_low, w_attend_out)
-    feed_low = root_norm(after_attend, norm_feed).astype(BF)
-    feed_rows = lax.all_gather(feed_low, "mp", axis=0, tiled=True)
-    gate_value = product(feed_rows, w_gate)
-    up_value = product(feed_rows, w_up)
-    sigmoid_gate = jax.nn.sigmoid(gate_value)
-    silu_gate = gate_value * sigmoid_gate
-    hidden_low = (silu_gate * up_value).astype(BF)
-    feed_out = lax.psum_scatter(
-        product(hidden_low, w_down).astype(BF), "mp", scatter_dimension=0, tiled=True
+    attend_low, qkv, attended_low, after_attend, feed_low = attend_forward(
+        local_in, norm_attend, norm_feed, w_attend
+    )
+    feed_parts, grad_feed_normed, grad_feed = feed_section(
+        12, feed_low, grad_feed_rows.reshape(-1, D), w_feed
+    )
+    units = grad_feed.shape[-1]
+    grad_feed = grad_feed.reshape(3, n_dp, D // n_dp, units).transpose(1, 0, 2, 3)
+    grad_feed = lax.psum_scatter(
+        grad_feed.reshape(3 * D, units), "dp", scatter_dimension=0, tiled=True
     ).astype(F32)
+    grad_gate, grad_up, grad_down = grad_feed.reshape(3, D // n_dp, units)
+    grad_down = grad_down.T
+    grad_local, grad_slots, grad_attend, grad_norm_attend, grad_norm_feed = attend_backward(
+        grad_feed_normed,
+        grad_final,
+        local_in,
+        after_attend,
+        attend_low,
+        qkv,
+        attended_low,
+        norm_attend,
+        norm_feed,
+        w_attend,
+    )
+    grad_norm_attend, grad_norm_feed = grad_norm_attend[0], grad_norm_feed[0]
+    grad_attend = lax.psum_scatter(
+        grad_attend, ("dp", "mp"), scatter_dimension=0, tiled=True
+    ).astype(F32)
+    feed_out = total(pair_sum(13, feed_parts.reshape(n_mp, rows, D)))
     out_bytes = ((after_attend + feed_out) * keep).astype(BF)[None]
 
-    grad_hidden = right_product(grad_feed_rows, w_down)
-    grad_down = left_product(hidden_low, grad_feed_rows)
-    grad_gate_low = (
-        grad_hidden * up_value * sigmoid_gate * (1.0 + gate_value * (1.0 - sigmoid_gate))
-    ).astype(BF)
-    grad_up_low = (grad_hidden * silu_gate).astype(BF)
-    grad_gate = left_product(feed_rows, grad_gate_low)
-    grad_up = left_product(feed_rows, grad_up_low)
-    grad_feed_normed = lax.psum_scatter(
-        (right_product(grad_gate_low, w_gate) + right_product(grad_up_low, w_up)).astype(BF),
-        "mp",
-        scatter_dimension=0,
-        tiled=True,
-    ).astype(F32)
-    grad_gate, grad_up, grad_down = (
-        lax.psum_scatter(grad_gate.astype(BF), "dp", scatter_dimension=0, tiled=True).astype(F32),
-        lax.psum_scatter(grad_up.astype(BF), "dp", scatter_dimension=0, tiled=True).astype(F32),
-        lax.psum_scatter(grad_down.astype(BF), "dp", scatter_dimension=1, tiled=True).astype(F32),
-    )
-    _, pull_feed = jax.vjp(root_norm, after_attend, norm_feed)
-    grad_after_norm, grad_norm_feed = pull_feed(grad_feed_normed)
-    grad_after = grad_final + grad_after_norm
-    grad_attend_low = grad_after.astype(BF)
-    grad_attend_out = left_product(attended_low, grad_attend_low)
-    grad_attended = right_product(grad_attend_low, w_attend_out)
-    _, pull_attend = jax.vjp(patch_attention, attend_proj)
-    (grad_proj,) = pull_attend(grad_attended)
-    grad_proj_low = grad_proj.astype(BF)
-    grad_attend_in = left_product(attend_low, grad_proj_low)
-    grad_attend_normed = right_product(grad_proj_low, w_attend)
-    _, pull_local = jax.vjp(root_norm, local_in, norm_attend)
-    grad_local_norm, grad_norm_attend = pull_local(grad_attend_normed)
-    grad_local = grad_after + grad_local_norm
-
     def owners(grad):
-        split = grad.reshape(n_dp, n_mp, -1, grad.shape[-1])
-        return split.transpose(1, 0, 2, 3).astype(BF)
-
-    grad_slots = grad_local.astype(BF).reshape(patches, n_dp, byte_cols).transpose(1, 0, 2)
-    grad_attend = owners(jnp.concatenate([grad_attend_in, grad_attend_out], axis=1))
-    grad_slots, grad_attend = exchange(
-        6, ("a2a", "dp", grad_slots), ("a2a", "mp", grad_attend)
-    )
+        return grad.astype(BF).reshape(n_dp, n_mp, -1, grad.shape[-1])
+
+    grad_slots = grad_slots.reshape(patches, n_dp, byte_cols).transpose(1, 0, 2)
+    (grad_slots,) = exchange(6, ("a2a", "dp", grad_slots))
     grad_slots = grad_slots.reshape(count, byte_cols)
     grad_patch_out = owners(left_product(global_low, grad_slots))
     parts = right_product(grad_slots, w_patch_out).astype(BF).reshape(n_dp, patches, D)
-    parts, grad_attend, grad_patch_out = exchange(
-        7,
-        ("a2a", "dp", parts),
-        ("a2a", "dp", total(grad_attend).astype(BF)),
-        ("a2a", "mp", grad_patch_out),
-    )
-    grad_attend = total(grad_attend)
+    parts, grad_patch_out = exchange(7, ("a2a", "dp", parts), ("a2a1", "mp", grad_patch_out))
     grad_global_out = total(parts)
     grad_mixer_low = grad_global_out.astype(BF)
     along = jnp.sum(grad_mixer_low.astype(F32) * unscaled, axis=1)
@@ -400,7 +872,7 @@
         9,
         ("a2a", "dp", parts),
         ("a2a", "mp", grad_mixer_out.reshape(n_mp, -1, D)),
-        ("a2a", "mp", grad_mixer_in),
+        ("a2a1", "mp", grad_mixer_in),
     )
     grad_mixer_out = total(grad_mixer_out).reshape(-1)
     _, pull_global = jax.vjp(root_norm, global_in, norm_global)

time: 1460 us -> 895 us (0.61)
  waiting for transfers between devices: 399 us -> 0.07 us
  matrix products: 249 us -> 59.4 us
  Pallas kernels: 549 us -> 710 us
  local copies, waits for them, and re-layouts: 135 us -> 49.9 us
  other arithmetic: 102 us -> 52.3 us
    reduce_scatter x4 -> x2, waiting for transfers between devices: 226 us -> 0.01 us  [the longest x1 0.01 us: body(): lax.psum_scatter(grad_feed.reshape(3 * D, units), 'dp', scatter_dimension...]
    pallas_call x0 -> x4, Pallas kernels: none -> 194 us  [the longest x1 77 us: feed_section(): pl.pallas_call(functools.partial(feed_kernel, n_mp), out_shape=[jax.Shape...]
    all_gather x7 -> x2, waiting for transfers between devices: 155 us -> 0.01 us  [the longest x1 0.01 us: body(): lax.all_gather(jnp.concatenate([attend_in.reshape(k_rows, -1), attend_out...]
    dot_general x6 -> x0, matrix products: 70.3 us -> none  [the longest x3 36.8 us: patch_attention(): result = jnp.einsum('phij,pjhd->pihd', probs, valued, precision=HIGH)]
    dot_general x9 -> x4, matrix products: 53.9 us -> 13.2 us  [product(): return jnp.dot(left, right, preferred_element_type=F32)]
    dot_general x9 -> x4, matrix products: 49.2 us -> 9.16 us  [left_product(): lax.dot_general(left, right, (((0,), (0,)), ((), ())), preferred_element_...]
    dot_general x9 -> x4, matrix products: 51.1 us -> 13.6 us  [right_product(): lax.dot_general(left, right, (((1,), (1,)), ((), ())), preferred_element_...]
    pallas_call x12, Pallas kernels: 549 us -> 516 us  [exchange(): pl.pallas_call(functools.partial(exchange_kernel, plan, sizes), out_shape...]
  transfers between devices with their start and end apart: 12 -> 4, of which waited for: 9 -> 0; matrix products, arithmetic and copies ran while one was open for 15% -> 17% of each run, Pallas kernels for 17% -> 71%
where the time goes in v2:
time: 895 us; the launch traced here: 887 us
  Pallas kernels  710 us (79%)
  matrix products  59.4 us (7%)
  other arithmetic  52.3 us (6%)
  local copies, waits for them, and re-layouts  49.9 us (6%)
  between operations  15 us (2%)
    pallas_call x12, Pallas kernels, exchange(): pl.pallas_call(functools.partial(exchange_kernel, plan, sizes), out_shape...  516 us
    pallas_call x1, Pallas kernels, feed_section(): pl.pallas_call(functools.partial(feed_kernel, n_mp), out_shape=[jax.Shape...  77 us
    pallas_call x1, Pallas kernels, attend_backward(): pl.pallas_call(attend_backward_kernel, out_shape=[jax.ShapeDtypeStruct((r...  52 us
    pallas_call x1, Pallas kernels, attend_forward(): pl.pallas_call(attend_forward_kernel, out_shape=[jax.ShapeDtypeStruct((ro...  33.5 us
    pallas_call x1, Pallas kernels, pair_sum(): pl.pallas_call(functools.partial(pair_sum_kernel, n_mp), out_shape=jax.Sh...  31.6 us
    dot_general x3, matrix products, gated_heads(): values = jnp.einsum('hts,shp->thp', weights, heads_x, precision=HIGH)  19.6 us
  transfers between devices with their start and end apart: 4, of which 0 were waited for; matrix products, arithmetic and copies ran while one was open for 17% of the time, Pallas kernels for 71%

profile of v2, /device:TPU:0, one launch (start us, length us, event | category | flops | bytes accessed | tf_op | source)
XLA Modules:
  0.0 887.0 jit_solution(11372781710554823430)
XLA Ops:
  11.1 2.0 pad_maximum_fusion
  19.6 2.3 fusion.41.refs_0_
  21.8 63.3 %shard_map.356 = (bf16[8,64,1024]{2,1,0:T(8,128)(2,1)}, bf16[8,32,896]{2,1,0:T(8,128)(2,1)}, bf16[8,32,1024]{2,1,0:T(8,128)(2,1)}, bf16[4,256,1024]{2,1,0:T(8,128)(2,1)}, bf16[4,64,1024]{2,1,0:T(8,128)(2,1)}) custom-call(bf16[8,64,1024]{2,1,0:T(8,128)(2,1)} %fusion.41.refs_0_, bf16[8,32,896]{2,1,0:T(8,128)(2,1)} %bitcast.225, ...), custom_call_target="tpu_custom_call" | custom-call | bytes 297795584 | tf_op jit(solution)/shard_map/pallas_call | solution.py:132
  85.1 4.5 convolution_convert_fusion.6
  89.6 52.9 %shard_map.357 = (bf16[8,64,1024]{2,1,0:T(8,128)(2,1)}, bf16[4,8,32,896]{3,2,1,0:T(8,128)(2,1)}, bf16[4,8,32,1024]{3,2,1,0:T(8,128)(2,1)}) custom-call(bf16[8,64,1024]{2,1,0:T(8,128)(2,1)} %bitcast.237, bf16[8,32,896]{2,1,0:T(8,128)(2,1)} %get-tuple-element.62.refs_1_, bf16[8,32,1024]{2,1,0:T(8,128)(2,1)} %get-tuple-element.63.refs_2_), custom_call_target="tpu_custom_call" | custom-call | bytes 318767104 | tf_op jit(solution)/shard_map/pallas_call | solution.py:132
  142.5 1.6 convert_reduce_fusion.5
  145.0 37.5 %shard_map.358 = bf16[8,64,1024]{2,1,0:T(8,128)(2,1)} custom-call(bf16[64,1024]{1,0:T(8,128)(2,1)} %multiply_convert_fusion.5.refs_0_), custom_call_target="tpu_custom_call" | custom-call | bytes 67108864 | tf_op jit(solution)/shard_map/pallas_call | solution.py:132
  182.5 1.5 copy.161
  184.0 3.1 fusion.94
  189.9 1.5 reduce-window.14
  192.0 1.6 fusion.44
  195.9 5.8 fusion.35
  205.2 3.3 copy.166
  212.4 64.2 %shard_map.359 = (bf16[8,64,1024]{2,1,0:T(8,128)(2,1)}, f32[8,8,128]{2,1,0:T(8,128)}, bf16[4,512,1024]{2,1,0:T(8,128)(2,1)}) custom-call(bf16[8,64,1024]{2,1,0:T(8,128)(2,1)} %bitcast.213, f32[8,8,128]{2,1,0:T(8,128)} %pad.49.refs_1_, bf16[512,1024]{1,0:T(8,128)(2,1)} %fusion.10.refs_2_.grad_final_ref), custom_call_target="tpu_custom_call" | custom-call | bytes 337641472 | tf_op jit(solution)/shard_map/pallas_call | solution.py:132
  280.2 27.6 %shard_map.360 = (bf16[8,64,1024]{2,1,0:T(8,128)(2,1)}, f32[8,8,128]{2,1,0:T(8,128)}) custom-call(bf16[64,1024]{1,0:T(8,128)(2,1)} %add_convert_fusion.refs_0_, f32[8,128]{1,0:T(8,128)} %pad_bitcast_fusion.2.refs_1_), custom_call_target="tpu_custom_call" | custom-call | bytes 69206016 | tf_op jit(solution)/shard_map/pallas_call | solution.py:132
  307.8 4.1 convolution_convert_fusion.4
  311.9 19.1 %shard_map.361 = bf16[8,64,1024]{2,1,0:T(8,128)(2,1)} custom-call(bf16[8,64,1024]{2,1,0:T(8,128)(2,1)} %bitcast.239), custom_call_target="tpu_custom_call" | custom-call | bytes 67108864 | tf_op jit(solution)/shard_map/pallas_call | solution.py:132
  331.1 1.5 convert_bitcast_fusion.3
  332.6 2.7 fusion.9.local_ref
  335.3 33.5 %shard_map.362 = (bf16[512,1024]{1,0:T(8,128)(2,1)}, bf16[512,3072]{1,0:T(8,128)(2,1)}, bf16[512,1024]{1,0:T(8,128)(2,1)}, f32[512,1024]{1,0:T(8,128)}, bf16[512,1024]{1,0:T(8,128)(2,1)}) custom-call(f32[512,1024]{1,0:T(8,128)} %fusion.9.local_ref, f32[1,1024]{1,0:T(1,128)} %bitcast.293, f32[1,1024]{1,0:T(1,128)} %bitcast.295, ...), custom_call_target="tpu_custom_call" | custom-call | flops 4294967296 | bytes 25165824 | tf_op jit(solution)/shard_map/pallas_call | solution.py:195
  368.9 77.0 %shard_map.363 = (bf16[2048,1024]{1,0:T(8,128)(2,1)}, f32[512,1024]{1,0:T(8,128)}, bf16[3,1024,1024]{2,1,0:T(8,128)(2,1)}) custom-call(bf16[512,1024]{1,0:T(8,128)(2,1)} %get-tuple-element.72.x_ref, bf16[2048,1024]{1,0:T(8,128)(2,1)} %bitcast.287, bf16[8,3,128,1024]{3,2,1,0:T(8,128)(2,1)} %bitcast.286), custom_call_target="tpu_custom_call" | custom-call | flops 38654705664 | bytes 31457280 | tf_op jit(solution)/shard_map/pallas_call | solution.py:503
  445.9 6.5 copy.183
  452.5 52.0 %shard_map.365 = (f32[512,1024]{1,0:T(8,128)}, bf16[512,1024]{1,0:T(8,128)(2,1)}, bf16[1024,4096]{1,0:T(8,128)(2,1)}, f32[1,1024]{1,0:T(1,128)}, f32[1,1024]{1,0:T(1,128)}) custom-call(f32[512,1024]{1,0:T(8,128)} %get-tuple-element.75.grad_feed_ref, bf16[512,1024]{1,0:T(8,128)(2,1)} %fusion.10.refs_2_.grad_final_ref, f32[512,1024]{1,0:T(8,128)} %fusion.9.local_ref, ...), custom_call_target="tpu_custom_call" | custom-call | flops 8589934592 | bytes 41943040 | tf_op jit(solution)/shard_map/pallas_call | solution.py:305
  505.5 2.8 copy.212
  508.3 26.4 %shard_map.366 = bf16[8,64,1024]{2,1,0:T(8,128)(2,1)} custom-call(bf16[8,64,1024]{2,1,0:T(8,128)(2,1)} %bitcast.211), custom_call_target="tpu_custom_call" | custom-call | bytes 67108864 | tf_op jit(solution)/shard_map/pallas_call | solution.py:132
  534.7 4.3 convolution_convert_fusion.3
  539.0 2.6 bitcast_convert_fusion.1
  541.6 38.3 %shard_map.367 = (bf16[8,64,1024]{2,1,0:T(8,128)(2,1)}, bf16[4,8,32,1024]{3,2,1,0:T(8,128)(2,1)}) custom-call(bf16[8,64,1024]{2,1,0:T(8,128)(2,1)} %bitcast.226, bf16[8,4,32,1024]{3,2,1,0:T(8,128)(2,1)} %bitcast.215), custom_call_target="tpu_custom_call" | custom-call | bytes 201326592 | tf_op jit(solution)/shard_map/pallas_call | solution.py:132
  579.9 2.9 reduce_sum.317.refs_2_
  585.7 51.8 %shard_map.368 = (bf16[8,64,1024]{2,1,0:T(8,128)(2,1)}, f32[8,8,128]{2,1,0:T(8,128)}, bf16[8,32,1024]{2,1,0:T(8,128)(2,1)}) custom-call(bf16[64,1024]{1,0:T(8,128)(2,1)} %get-tuple-element.217.refs_0_, f32[8,128]{1,0:T(8,128)} %pad_bitcast_fusion.1.refs_1_, bf16[8,32,1024]{2,1,0:T(8,128)(2,1)} %reduce_sum.317.refs_2_), custom_call_target="tpu_custom_call" | custom-call | bytes 102760448 | tf_op jit(solution)/shard_map/pallas_call | solution.py:132
  638.4 3.4 multiply_reduce_fusion.7
  641.7 2.0 copy.172
  643.8 6.2 fusion.32
  649.9 2.0 copy.173
  652.0 7.7 fusion.7
  660.7 1.8 fusion.64
  663.6 5.1 reduce-window.16
  673.3 2.5 convolution_convert_fusion
  675.8 2.3 convolution_convert_fusion.2
  678.1 59.1 %shard_map.369 = (bf16[8,64,1024]{2,1,0:T(8,128)(2,1)}, bf16[4,64,1024]{2,1,0:T(8,128)(2,1)}, bf16[4,8,32,896]{3,2,1,0:T(8,128)(2,1)}) custom-call(bf16[8,64,1024]{2,1,0:T(8,128)(2,1)} %bitcast.235, bf16[4,64,1024]{2,1,0:T(8,128)(2,1)} %bitcast.219, bf16[8,4,32,896]{3,2,1,0:T(8,128)(2,1)} %bitcast.224), custom_call_target="tpu_custom_call" | custom-call | bytes 218103808 | tf_op jit(solution)/shard_map/pallas_call | solution.py:132
  737.3 2.7 reduce_sum.389.refs_2_
  743.3 37.3 %shard_map.370 = (bf16[8,64,1024]{2,1,0:T(8,128)(2,1)}, f32[4,136,128]{2,1,0:T(8,128)}, bf16[8,32,896]{2,1,0:T(8,128)(2,1)}) custom-call(bf16[64,1024]{1,0:T(8,128)(2,1)} %fusion.50.refs_0_, f32[136,128]{1,0:T(8,128)} %pad_bitcast_fusion.refs_1_, bf16[8,32,896]{2,1,0:T(8,128)(2,1)} %reduce_sum.389.refs_2_), custom_call_target="tpu_custom_call" | custom-call | bytes 114294784 | tf_op jit(solution)/shard_map/pallas_call | solution.py:132
  783.3 31.6 %shard_map.364 = bf16[2,512,1024]{2,1,0:T(8,128)(2,1)} custom-call(bf16[4,512,1024]{2,1,0:T(8,128)(2,1)} %bitcast.210), custom_call_target="tpu_custom_call" | custom-call | bytes 134217728 | tf_op jit(solution)/shard_map/pallas_call | solution.py:590
  815.6 3.6 convolution_convert_fusion.1
  819.2 2.7 bitcast_convert_fusion
  821.9 38.5 %shard_map.371 = (bf16[8,64,1024]{2,1,0:T(8,128)(2,1)}, bf16[4,256,1024]{2,1,0:T(8,128)(2,1)}, f32[8,136,128]{2,1,0:T(8,128)}) custom-call(bf16[8,64,1024]{2,1,0:T(8,128)(2,1)} %bitcast.236, bf16[4,256,1024]{2,1,0:T(8,128)(2,1)} %bitcast.214, f32[136,128]{1,0:T(8,128)} %reduce_sum.390.refs_2_), custom_call_target="tpu_custom_call" | custom-call | bytes 236978176 | tf_op jit(solution)/shard_map/pallas_call | solution.py:132
  860.4 2.2 convert_reduce_fusion
  871.1 3.1 fusion.42
  (248 shorter events, 59.8 us)
Async XLA Ops:
  7.2 6.0 copy-start.27
  7.2 328.1 %all-gather.4.cloned.1.call-start = ((), (), s32[]{:S(2)}) async-start(), calls=%async_computation.2 | async-start | bytes 8650752 | tf_op jit(solution)/shard_map/all_gather | solution.py:711
  9.9 4.0 copy-start.23
  9.9 358.9 %all-gather.6.cloned.1.call-start = ((), (), s32[]{:S(2)}) async-start(), calls=%async_computation.5 | async-start | bytes 7077888 | tf_op jit(solution)/shard_map/all_gather | solution.py:717
  13.1 2.2 copy-start.24
  13.1 3.2 copy-start.31
  13.2 861.0 %reduce-scatter.5.cloned.1.call-start = ((), (), s32[]{:S(2)}) async-start(), calls=%async_computation.4 | async-start | bytes 7077888 | tf_op jit(solution)/shard_map/reduce_scatter | solution.py:801
  14.2 3.8 copy-start.40
  14.2 5.1 copy-start.4
  89.6 54.7 %copy-start.32 = (f32[1024]{0:T(1024)S(1)}, f32[1024]{0:T(1024)}, u32[]{:S(2)}) copy-start(f32[1024]{0:T(1024)} %param.32) | copy-start | bytes 12292
  142.5 40.0 %copy-start.12 = (bf16[4,8,32,896]{3,2,1,0:T(8,128)(2,1)S(1)}, bf16[4,8,32,896]{3,2,1,0:T(8,128)(2,1)}, u32[]{:S(2)}) copy-start(bf16[4,8,32,896]{3,2,1,0:T(8,128)(2,1)} %get-tuple-element.65) | copy-start | bytes 5505028
  187.1 4.9 copy-start.1
  187.1 4.7 slice-start.2
  187.1 4.7 slice-start.3
  187.1 4.7 slice-start
  187.2 4.8 slice-start.1
  191.9 2.8 copy-start.42
  194.9 6.9 copy-start.29
  195.9 5.8 copy-start.17
  203.0 5.5 copy-start.8
  205.2 4.6 copy-start.26
  208.5 2.7 copy-start.14
  452.4 425.2 %reduce-scatter.3.cloned.1.call-start = ((), (), s32[]{:S(2)}) async-start(), calls=%async_computation.3 | async-start | bytes 8650752 | tf_op jit(solution)/shard_map/reduce_scatter | solution.py:819
  534.6 4.3 copy-start.19
  534.6 4.3 copy-start.38
  638.4 5.4 copy-start.30
  652.0 10.5 %copy-start.7 = (f32[512,256]{1,0:T(8,128)S(1)}, f32[512,256]{1,0:T(8,128)}, u32[]{:S(2)}) copy-start(f32[512,256]{1,0:T(8,128)} %copy.173) | copy-start | bytes 1572868
  659.7 2.9 copy-start.2
  659.7 2.9 copy-start.6
  670.0 1.9 copy-start.18
  670.5 2.8 copy-start.16
  670.5 2.8 copy-start.43
  673.3 2.5 copy-start.11
  737.2 3.8 copy-start.15
  737.3 4.5 copy-start.33
  737.3 4.5 copy-start.34
  783.3 31.7 %copy-start.28 = (f32[4,136,128]{2,1,0:T(8,128)S(1)}, f32[4,136,128]{2,1,0:T(8,128)}, u32[]{:S(2)}) copy-start(f32[4,136,128]{2,1,0:T(8,128)} %get-tuple-element.91) | copy-start | bytes 835588
  783.3 32.3 %copy-start.36 = (bf16[4,256,1024]{2,1,0:T(8,128)(2,1)S(1)}, bf16[4,256,1024]{2,1,0:T(8,128)(2,1)}, u32[]{:S(2)}) copy-start(bf16[4,256,1024]{2,1,0:T(8,128)(2,1)} %get-tuple-element.61) | copy-start | bytes 6291460
  815.6 3.6 copy-start.37
  815.6 3.6 copy-start.39
  860.4 3.4 copy-start.20
  862.6 2.5 copy-start.22
  862.6 3.4 copy-start.21
  866.1 1.8 copy-start
  867.9 2.9 copy-start.13
  867.9 3.2 copy-start.10
  868.3 2.7 copy-start.9
  874.2 2.4 copy-start.3
  (4 other events, 4.3 us)
Sparse Core Ops, SparseCore 0:
  11.5 119.3 all-gather.3
  133.1 143.2 all-gather.5
  452.6 147.8 reduce-scatter.4
  602.6 161.7 reduce-scatter.2
